TPU v7x, 32 devices: a whole 2x2x4 slice. The times are simulated.
32 devices in a mesh: dp: 8 (over z, x), tensor: 4 (over y, core).
Axes of the slice: x: 2, y: 2, z: 4, core: 2. Of those that a mesh axis runs over, the one named last changes fastest.
Arguments:
- inputs: bfloat16 [8192, 640], P('dp'), may hold values from -6 to 6
- cotangent: bfloat16 [8192, 640], P('dp'), may hold values from -6 to 6
- seq_lengths: int32 [3], replicated, may hold values from 1024 to 4096, as said below
- w_query: float32 [640, 1024], P('dp', 'tensor'), may hold values from -0.25 to 0.25
- w_kv: float32 [640, 512], P('dp'), may hold values from -0.25 to 0.25
- w_out: float32 [1024, 640], P('tensor', 'dp'), may hold values from -0.1875 to 0.1875
- w_gate_up: float32 [2, 640, 2048], P(None, 'dp', 'tensor'), may hold values from -0.25 to 0.25
- w_down: float32 [2048, 640], P('tensor', 'dp'), may hold values from -0.125 to 0.125
- gains: float32 [3072], P('dp'), may hold values from -0.3 to 0.6
- mom_query: float32 [640, 1024], P('dp', 'tensor'), may hold values from -160 to 160
- mom_kv: float32 [640, 512], P('dp'), may hold values from -160 to 160
- mom_out: float32 [1024, 640], P('tensor', 'dp'), may hold values from -160 to 160
- mom_gate_up: float32 [2, 640, 2048], P(None, 'dp', 'tensor'), may hold values from -160 to 160
- mom_down: float32 [2048, 640], P('tensor', 'dp'), may hold values from -160 to 160
- mom_gains: float32 [3072], P('dp'), may hold values from -160 to 160
Outputs:
- output: bfloat16 [8192, 640], P('dp')
- grad_input: float32 [8192, 640], P('dp')
- grad_query: float32 [640, 1024], P('dp', 'tensor')
- grad_kv: float32 [640, 512], P('dp')
- grad_out: float32 [1024, 640], P('tensor', 'dp')
- grad_gate_up: float32 [2, 640, 2048], P(None, 'dp', 'tensor')
- grad_down: float32 [2048, 640], P('tensor', 'dp')
- grad_gains: float32 [3072], P('dp')
- new_query: float32 [640, 1024], P('dp', 'tensor')
- new_kv: float32 [640, 512], P('dp')
- new_out: float32 [1024, 640], P('tensor', 'dp')
- new_gate_up: float32 [2, 640, 2048], P(None, 'dp', 'tensor')
- new_down: float32 [2048, 640], P('tensor', 'dp')
- new_gains: float32 [3072], P('dp')
- new_mom_query: float32 [640, 1024], P('dp', 'tensor')
- new_mom_kv: float32 [640, 512], P('dp')
- new_mom_out: float32 [1024, 640], P('tensor', 'dp')
- new_mom_gate_up: float32 [2, 640, 2048], P(None, 'dp', 'tensor')
- new_mom_down: float32 [2048, 640], P('tensor', 'dp')
- new_mom_gains: float32 [3072], P('dp')
Inputs may be any that keep to these rules, and one draw needn't show every extreme that they name: `seq_lengths`: the 3 sequences lie end to end in token order and their lengths sum to 8192; exactly one is 4096 tokens long, and the shortest is exactly 1024 tokens.
All inputs are finite; a program needn't handle non-finite values.
Results may differ from a plain program's by a relative error of at most 0.024.
Values may be sent and summed in bfloat16 or wider, within the bound.
A program may use at most 128 MiB of HBM per device.

v0:
```python
import math

import jax
import jax.numpy as jnp
from jax import lax
from jax.sharding import PartitionSpec as P

WINDOW = 512
QB = 512
NS_ITERS = 5


EPSILON = 1e-06
MOMENTUM = 0.95
MUON_RATE = 0.5
ROPE_BASE = 10000.0
COEF_FIRST = 3.4445
COEF_SECOND = -4.775
COEF_THIRD = 2.0315
MASKED = -1e30
HIGHEST = lax.Precision.HIGHEST


def from_behind(block, axis, distance):
    devices = range(lax.axis_size(axis))
    route = [(i - distance, i) for i in devices if i - distance in devices]
    return lax.ppermute(block, axis, route)


def rms_scale(values, scale_gain):
    inverse = lax.rsqrt(jnp.mean(values * values, axis=-1, keepdims=True) + EPSILON)
    return values * inverse * (1.0 + scale_gain)


def rotate(values, position):
    half_dim = values.shape[-1] // 2
    exponent = jnp.arange(half_dim).astype(jnp.float32) * (-2.0 / values.shape[-1])
    frequency = jnp.power(ROPE_BASE, exponent)
    angles = position.astype(jnp.float32)[:, None] * frequency[None, :]
    cosine = jnp.cos(angles)
    sine_vals = jnp.sin(angles)
    first_half = values[..., :half_dim]
    second_half = values[..., half_dim:]
    return jnp.concatenate(
        [
            first_half * cosine - second_half * sine_vals,
            second_half * cosine + first_half * sine_vals,
        ],
        axis=-1,
    )


def orthogonalize(matrix):
    row_count, col_count = matrix.shape
    flipped = row_count > col_count
    current = matrix.T if flipped else matrix
    current = current / (jnp.sqrt(jnp.sum(current * current)) + 1e-07)
    for sweep_index in range(NS_ITERS):
        square = jnp.dot(current, current.T, precision=HIGHEST)
        polynomial = COEF_SECOND * square + COEF_THIRD * jnp.dot(square, square, precision=HIGHEST)
        current = COEF_FIRST * current + jnp.dot(polynomial, current, precision=HIGHEST)
    result = current.T if flipped else current
    return result * (MUON_RATE * math.sqrt(max(1.0, row_count / col_count)))


def shards(
    inputs,
    cotangent,
    seq_lengths,
    w_query,
    w_kv,
    w_out,
    w_gate_up,
    w_down,
    gains,
    mom_query,
    mom_kv,
    mom_out,
    mom_gate_up,
    mom_down,
    mom_gains,
):
    low_type = jnp.bfloat16
    full_type = jnp.float32
    row_count = inputs.shape[0]
    model_width = inputs.shape[1]
    head_dim = w_kv.shape[1] // 2
    hidden_units = w_down.shape[0]
    dp_count = lax.axis_size("dp")
    dp_index = lax.axis_index("dp")
    tensor_count = lax.axis_size("tensor")
    tensor_index = lax.axis_index("tensor")
    share_rows = row_count // tensor_count
    share_start = tensor_index * share_rows
    score_scale = head_dim ** (-0.5)
    query_weight, kv_weight, out_weight, gate_up_weight, down_weight, gain_low = (
        lax.all_gather(w_query.astype(low_type), "dp", axis=0, tiled=True),
        lax.all_gather(w_kv.astype(low_type), "dp", axis=0, tiled=True),
        lax.all_gather(w_out.astype(low_type), "dp", axis=1, tiled=True),
        lax.all_gather(w_gate_up.astype(low_type), "dp", axis=1, tiled=True),
        lax.all_gather(w_down.astype(low_type), "dp", axis=1, tiled=True),
        lax.all_gather(gains.astype(low_type), "dp", axis=0, tiled=True),
    )
    gain_vals = gain_low.astype(full_type)
    gain_in = gain_vals[0:model_width]
    gain_attn = gain_vals[model_width : 2 * model_width]
    gain_pre = gain_vals[2 * model_width : 3 * model_width]
    gain_post = gain_vals[3 * model_width : 4 * model_width]
    gain_query = gain_vals[4 * model_width : 4 * model_width + head_dim]
    gain_key = gain_vals[4 * model_width + head_dim :]
    ext_places = dp_index * row_count - WINDOW + jnp.arange(row_count + WINDOW, dtype=jnp.int32)
    seq_ends = jnp.cumsum(seq_lengths)
    passed = ext_places[:, None] >= seq_ends[None, :]
    segment = jnp.sum(passed.astype(jnp.int32), axis=1)
    seq_starts = jnp.sum(jnp.where(passed, seq_lengths[None, :], 0), axis=1)
    segment = jnp.where(ext_places < 0, -1, segment)
    own_position = (ext_places - seq_starts)[WINDOW:]

    def block_mask(start):
        place_query = ext_places[WINDOW + start : WINDOW + start + QB]
        place_key = ext_places[start : start + QB + WINDOW]
        seg_query = segment[WINDOW + start : WINDOW + start + QB]
        seg_key = segment[start : start + QB + WINDOW]
        place_gap = place_query[:, None] - place_key[None, :]
        return (seg_query[:, None] == seg_key[None, :]) & (place_gap >= 0) & (place_gap < WINDOW)

    def rope_norm(raw_rows, scale_gain):
        return rotate(rms_scale(raw_rows, scale_gain), own_position)

    def activate(raw_rows):
        return (
            jax.nn.gelu(raw_rows[:, :hidden_units], approximate=True) * raw_rows[:, hidden_units:]
        )

    gate_up_cat = jnp.concatenate([gate_up_weight[0], gate_up_weight[1]], axis=1)
    inputs_f = inputs.astype(full_type)
    back_out = cotangent.astype(full_type)
    normed_f, input_norm_back = jax.vjp(rms_scale, inputs_f, gain_in)
    normed = normed_f.astype(low_type)
    proj_weight = jnp.concatenate([query_weight, kv_weight], axis=1)
    proj_raw = jnp.dot(normed, proj_weight, preferred_element_type=full_type)
    queries_f, query_back = jax.vjp(rope_norm, proj_raw[:, :head_dim], gain_query)
    keys_f, key_back = jax.vjp(rope_norm, proj_raw[:, head_dim : 2 * head_dim], gain_key)
    queries = queries_f.astype(low_type)
    key_rows = keys_f.astype(low_type)
    value_rows = proj_raw[:, 2 * head_dim :].astype(low_type)
    halo_keys, halo_values = from_behind(
        (key_rows[row_count - WINDOW :], value_rows[row_count - WINDOW :]), "dp", 1
    )
    ext_keys = jnp.concatenate([halo_keys, key_rows], axis=0)
    ext_values = jnp.concatenate([halo_values, value_rows], axis=0)
    block_count = row_count // QB
    attended_parts = []
    log_parts = []
    for block_index in range(block_count):
        start = block_index * QB
        allowed = block_mask(start)
        scores = (
            jnp.einsum(
                "qd,kd->qk",
                queries[start : start + QB],
                ext_keys[start : start + QB + WINDOW],
                preferred_element_type=full_type,
            )
            * score_scale
        )
        scores = jnp.where(allowed, scores, MASKED)
        row_max = jnp.max(scores, axis=1, keepdims=True)
        weights = jnp.exp(scores - row_max)
        totals = jnp.sum(weights, axis=1, keepdims=True)
        attn_probs = (weights / totals).astype(low_type)
        attended_parts.append(
            jnp.dot(
                attn_probs,
                ext_values[start : start + QB + WINDOW],
                preferred_element_type=full_type,
            )
        )
        log_parts.append(row_max + jnp.log(totals))
    attended = jnp.concatenate(attended_parts, axis=0).astype(low_type)
    log_totals = jnp.concatenate(log_parts, axis=0)
    attn_part = jnp.dot(attended, out_weight, preferred_element_type=full_type)
    inputs_share = lax.dynamic_slice_in_dim(inputs_f, share_start, share_rows, 0)
    back_share = lax.dynamic_slice_in_dim(back_out, share_start, share_rows, 0)
    attn_share = lax.psum_scatter(
        attn_part.astype(jnp.bfloat16), "tensor", scatter_dimension=0, tiled=True
    ).astype(jnp.float32)
    branch_attn, attn_norm_back = jax.vjp(rms_scale, attn_share, gain_attn)
    hidden_share = inputs_share + branch_attn
    ffn_share, pre_norm_back = jax.vjp(rms_scale, hidden_share, gain_pre)
    ffn_in = lax.all_gather(ffn_share.astype(low_type), "tensor", axis=0, tiled=True)
    gate_up_raw = jnp.dot(ffn_in, gate_up_cat, preferred_element_type=full_type)
    mixed_f, activate_back = jax.vjp(activate, gate_up_raw)
    mixed_rows = mixed_f.astype(low_type)
    down_part = jnp.dot(mixed_rows, down_weight, preferred_element_type=full_type)
    mixed, activate_back, down_part = (mixed_rows, activate_back, down_part)
    down_share = lax.psum_scatter(
        down_part.astype(jnp.bfloat16), "tensor", scatter_dimension=0, tiled=True
    ).astype(jnp.float32)
    branch_ffn, post_norm_back = jax.vjp(rms_scale, down_share, gain_post)
    output_share = (hidden_share + branch_ffn).astype(low_type)
    back_down_share, grad_gain_post = post_norm_back(back_share)
    output, back_down = (
        lax.all_gather(output_share, "tensor", axis=0, tiled=True),
        lax.all_gather(back_down_share.astype(low_type), "tensor", axis=0, tiled=True),
    )
    grad_down_part = jnp.einsum("tf,td->fd", mixed, back_down, preferred_element_type=full_type)
    back_mixed = jnp.einsum("td,fd->tf", back_down, down_weight, preferred_element_type=full_type)
    (back_gate_up_f,) = activate_back(back_mixed)
    back_gate_up = back_gate_up_f.astype(low_type)
    grad_cat = jnp.einsum("td,tf->df", ffn_in, back_gate_up, preferred_element_type=full_type)
    grad_gate_up_part = jnp.stack([grad_cat[:, :hidden_units], grad_cat[:, hidden_units:]], axis=0)
    back_ffn_part = jnp.einsum(
        "tf,df->td", back_gate_up, gate_up_cat, preferred_element_type=full_type
    )
    grad_down_local, grad_gate_up_local, back_ffn_part = (
        grad_down_part,
        grad_gate_up_part,
        back_ffn_part,
    )
    back_ffn_share = lax.psum_scatter(
        back_ffn_part.astype(jnp.bfloat16), "tensor", scatter_dimension=0, tiled=True
    ).astype(jnp.float32)
    back_pre, grad_gain_pre = pre_norm_back(back_ffn_share)
    back_hidden = back_share + back_pre
    back_attn_share, grad_gain_attn = attn_norm_back(back_hidden)
    back_attn = lax.all_gather(back_attn_share.astype(low_type), "tensor", axis=0, tiled=True)
    grad_out_local = jnp.einsum("th,td->hd", attended, back_attn, preferred_element_type=full_type)
    back_attended = jnp.einsum(
        "td,hd->th", back_attn, out_weight, preferred_element_type=full_type
    ).astype(low_type)
    query_parts = []
    back_ext_keys = jnp.zeros((row_count + WINDOW, head_dim), full_type)
    back_ext_values = jnp.zeros((row_count + WINDOW, head_dim), full_type)
    for block_index in range(block_count):
        start = block_index * QB
        allowed = block_mask(start)
        query_block = queries[start : start + QB]
        key_block = ext_keys[start : start + QB + WINDOW]
        value_block = ext_values[start : start + QB + WINDOW]
        scores = (
            jnp.einsum("qd,kd->qk", query_block, key_block, preferred_element_type=full_type)
            * score_scale
        )
        scores = jnp.where(allowed, scores, MASKED)
        attn_probs = jnp.exp(scores - log_totals[start : start + QB])
        probs_low = attn_probs.astype(low_type)
        back_block = back_attended[start : start + QB]
        back_probs = jnp.einsum(
            "qd,kd->qk", back_block, value_block, preferred_element_type=full_type
        )
        row_dot = jnp.sum(attn_probs * back_probs, axis=1, keepdims=True)
        back_scores = (attn_probs * (back_probs - row_dot)).astype(low_type)
        query_parts.append(
            jnp.dot(back_scores, key_block, preferred_element_type=full_type) * score_scale
        )
        back_ext_keys = back_ext_keys.at[start : start + QB + WINDOW].add(
            jnp.einsum("qk,qd->kd", back_scores, query_block, preferred_element_type=full_type)
            * score_scale
        )
        back_ext_values = back_ext_values.at[start : start + QB + WINDOW].add(
            jnp.einsum("qk,qd->kd", probs_low, back_block, preferred_element_type=full_type)
        )
    next_keys, next_values = (
        from_behind(back_ext_keys[:WINDOW].astype(jnp.bfloat16), "dp", -1).astype(jnp.float32),
        from_behind(back_ext_values[:WINDOW].astype(jnp.bfloat16), "dp", -1).astype(jnp.float32),
    )
    back_keys = back_ext_keys[WINDOW:].at[row_count - WINDOW :].add(next_keys)
    back_values = back_ext_values[WINDOW:].at[row_count - WINDOW :].add(next_values)
    back_queries = jnp.concatenate(query_parts, axis=0)
    back_query_raw_f, gain_query_part = query_back(back_queries)
    back_query_raw = back_query_raw_f.astype(low_type)
    grad_query_local = jnp.einsum(
        "td,th->dh", normed, back_query_raw, preferred_element_type=full_type
    )
    normed_part = jnp.einsum(
        "th,dh->td", back_query_raw, query_weight, preferred_element_type=full_type
    )
    normed_sum, key_sum, value_sum, gain_query_sum = (
        lax.psum(normed_part.astype(jnp.bfloat16), "tensor").astype(jnp.float32),
        lax.psum(back_keys.astype(jnp.bfloat16), "tensor").astype(jnp.float32),
        lax.psum(back_values.astype(jnp.bfloat16), "tensor").astype(jnp.float32),
        lax.psum(gain_query_part.astype(jnp.bfloat16), "tensor").astype(jnp.float32),
    )
    back_key_raw_f, grad_gain_key = key_back(key_sum)
    back_kv = jnp.concatenate([back_key_raw_f, value_sum], axis=1).astype(low_type)
    grad_kv_local = jnp.einsum("td,tk->dk", normed, back_kv, preferred_element_type=full_type)
    back_normed = normed_sum + jnp.einsum(
        "tk,dk->td", back_kv, kv_weight, preferred_element_type=full_type
    )
    back_in, grad_gain_in = input_norm_back(back_normed)
    grad_share = back_hidden + lax.dynamic_slice_in_dim(back_in, share_start, share_rows, 0)
    gain_share = jnp.concatenate([grad_gain_attn, grad_gain_pre, grad_gain_post])
    grad_input, gain_gathered = (
        lax.all_gather(grad_share.astype(jnp.bfloat16), "tensor", axis=0, tiled=True).astype(
            grad_share.dtype
        ),
        lax.all_gather(gain_share.astype(jnp.bfloat16), "tensor", axis=0, tiled=True).astype(
            gain_share.dtype
        ),
    )
    gain_summed = jnp.sum(gain_gathered.reshape(tensor_count, 3 * model_width), axis=0)
    grad_gain_attn = gain_summed[0:model_width]
    grad_gain_pre = gain_summed[model_width : 2 * model_width]
    grad_gain_post = gain_summed[2 * model_width :]
    grad_gains_local = jnp.concatenate(
        [grad_gain_in, grad_gain_attn, grad_gain_pre, grad_gain_post, gain_query_sum, grad_gain_key]
    )
    grad_query, grad_kv, grad_out, grad_gate_up, grad_down, grad_gains = (
        lax.psum_scatter(grad_query_local, "dp", scatter_dimension=0, tiled=True),
        lax.psum_scatter(grad_kv_local, "dp", scatter_dimension=0, tiled=True),
        lax.psum_scatter(grad_out_local, "dp", scatter_dimension=1, tiled=True),
        lax.psum_scatter(grad_gate_up_local, "dp", scatter_dimension=1, tiled=True),
        lax.psum_scatter(grad_down_local, "dp", scatter_dimension=1, tiled=True),
        lax.psum_scatter(grad_gains_local, "dp", scatter_dimension=0, tiled=True),
    )
    new_mom_query = MOMENTUM * mom_query + grad_query
    new_mom_kv = MOMENTUM * mom_kv + grad_kv
    new_mom_out = MOMENTUM * mom_out + grad_out
    new_mom_gate_up = MOMENTUM * mom_gate_up + grad_gate_up
    new_mom_down = MOMENTUM * mom_down + grad_down
    new_mom_gains = MOMENTUM * mom_gains + grad_gains
    nest_query = grad_query + MOMENTUM * new_mom_query
    nest_kv = grad_kv + MOMENTUM * new_mom_kv
    nest_out = grad_out + MOMENTUM * new_mom_out
    nest_gate_up = grad_gate_up + MOMENTUM * new_mom_gate_up
    nest_down = grad_down + MOMENTUM * new_mom_down
    nest_gains = grad_gains + MOMENTUM * new_mom_gains
    new_gains = gains - 0.1 / math.sqrt(row_count * dp_count) * nest_gains
    whole_query, whole_kv, whole_out, whole_gate_up, whole_down = (
        lax.all_gather(nest_query.astype(jnp.bfloat16), "dp", axis=0, tiled=True).astype(
            nest_query.dtype
        ),
        lax.all_gather(nest_kv.astype(jnp.bfloat16), "dp", axis=0, tiled=True).astype(
            nest_kv.dtype
        ),
        lax.all_gather(nest_out.astype(jnp.bfloat16), "dp", axis=1, tiled=True).astype(
            nest_out.dtype
        ),
        lax.all_gather(nest_gate_up.astype(jnp.bfloat16), "dp", axis=1, tiled=True).astype(
            nest_gate_up.dtype
        ),
        lax.all_gather(nest_down.astype(jnp.bfloat16), "dp", axis=1, tiled=True).astype(
            nest_down.dtype
        ),
    )
    matrices = [
        whole_query,
        whole_kv[:, :head_dim],
        whole_kv[:, head_dim:],
        whole_out,
        whole_gate_up[0],
        whole_gate_up[1],
        whole_down,
    ]
    steps_list = [orthogonalize(matrix) for matrix in matrices]
    shard_rows = model_width // dp_count
    offset = dp_index * shard_rows
    step_query = lax.dynamic_slice_in_dim(steps_list[0], offset, shard_rows, 0)
    step_kv = lax.dynamic_slice_in_dim(
        jnp.concatenate(steps_list[1:3], axis=1), offset, shard_rows, 0
    )
    step_out = lax.dynamic_slice_in_dim(steps_list[3], offset, shard_rows, 1)
    step_gate_up = lax.dynamic_slice_in_dim(
        jnp.stack(steps_list[4:6], axis=0), offset, shard_rows, 1
    )
    step_down = lax.dynamic_slice_in_dim(steps_list[6], offset, shard_rows, 1)
    new_query = w_query - step_query
    new_kv = w_kv - step_kv
    new_out = w_out - step_out
    new_gate_up = w_gate_up - step_gate_up
    new_down = w_down - step_down
    return (
        output,
        grad_input,
        grad_query,
        grad_kv,
        grad_out,
        grad_gate_up,
        grad_down,
        grad_gains,
        new_query,
        new_kv,
        new_out,
        new_gate_up,
        new_down,
        new_gains,
        new_mom_query,
        new_mom_kv,
        new_mom_out,
        new_mom_gate_up,
        new_mom_down,
        new_mom_gains,
    )


def solution(mesh):
    return jax.shard_map(
        shards,
        mesh=mesh,
        in_specs=(
            P("dp", None),
            P("dp", None),
            P(),
            P("dp", "tensor"),
            P("dp", None),
            P("tensor", "dp"),
            P(None, "dp", "tensor"),
            P("tensor", "dp"),
            P("dp"),
            P("dp", "tensor"),
            P("dp", None),
            P("tensor", "dp"),
            P(None, "dp", "tensor"),
            P("tensor", "dp"),
            P("dp"),
        ),
        out_specs=(
            P("dp", None),
            P("dp", None),
            P("dp", "tensor"),
            P("dp", None),
            P("tensor", "dp"),
            P(None, "dp", "tensor"),
            P("tensor", "dp"),
            P("dp"),
            P("dp", "tensor"),
            P("dp", None),
            P("tensor", "dp"),
            P(None, "dp", "tensor"),
            P("tensor", "dp"),
            P("dp"),
            P("dp", "tensor"),
            P("dp", None),
            P("tensor", "dp"),
            P(None, "dp", "tensor"),
            P("tensor", "dp"),
            P("dp"),
        ),
        check_vma=False,
    )
```

profile of v0, /device:TPU:0, one launch (start us, length us, event | category | flops | bytes accessed | tf_op | source)
XLA Modules:
  0.0 856.1 jit_solution(3182146237653519884)
XLA Ops:
  11.2 27.7 %all-gather = bf16[8,1,384]{2,1,0:T(2,128)(2,1)S(1)} all-gather(bf16[1,1,384]{2,1,0:T(2,128)(2,1)S(1)} %reshape.393), channel_id=1, replica_groups=mesh['dp'=8,'tensor'=4] {'dp'}, dimensions={0}, use_global_device_ids=true | all-gather | bytes 6912 | tf_op jit(solution)/shard_map/all_gather | solution.py:102
  39.5 30.9 %all_gather.52 = bf16[640,256]{1,0:T(8,128)(2,1)S(1)} all-gather(bf16[80,256]{1,0:T(8,128)(2,1)S(1)} %convert_element_type.183), channel_id=1, replica_groups=mesh['dp'=8,'tensor'=4] {'dp'}, dimensions={0}, use_global_device_ids=true | all-gather | bytes 368640 | tf_op jit(solution)/shard_map/all_gather | solution.py:97
  70.4 31.6 %all_gather.53 = bf16[640,512]{1,0:T(8,128)(2,1)S(1)} all-gather(bf16[80,512]{1,0:T(8,128)(2,1)S(1)} %convert_element_type.184), channel_id=1, replica_groups=mesh['dp'=8,'tensor'=4] {'dp'}, dimensions={0}, use_global_device_ids=true | all-gather | bytes 737280 | tf_op jit(solution)/shard_map/all_gather | solution.py:98
  105.6 2.3 collective-permute-start.1
  109.7 2.4 fusion.150
  118.5 30.9 %all_gather.54 = bf16[256,640]{0,1:T(8,128)(2,1)S(1)} all-gather(bf16[256,80]{0,1:T(8,128)(2,1)S(1)} %convert_element_type.189), channel_id=1, replica_groups=mesh['dp'=8,'tensor'=4] {'dp'}, dimensions={1}, use_global_device_ids=true | all-gather | bytes 368640 | tf_op jit(solution)/shard_map/all_gather | solution.py:99
  156.1 3.0 convert_element_type.178
  159.1 21.9 %reduce-scatter.9.cloned.1.call-done = bf16[256,640]{1,0:T(8,128)(2,1)} async-done(((bf16[1024,640]{1,0:T(8,128)(2,1)}), bf16[256,640]{1,0:T(8,128)(2,1)}) %reduce-scatter.9.cloned.1.call-update) | async-done | bytes 327696 | tf_op jit(solution)/shard_map/reduce_scatter | solution.py:185
  185.6 34.9 %all_gather.57 = bf16[512,640]{0,1:T(8,128)(2,1)} all-gather(bf16[512,80]{0,1:T(8,128)(2,1)S(1)} %convert_element_type.195), channel_id=1, replica_groups=mesh['dp'=8,'tensor'=4] {'dp'}, dimensions={1}, use_global_device_ids=true | all-gather | bytes 737280 | tf_op jit(solution)/shard_map/all_gather | solution.py:101
  220.5 2.4 slice_bitcast_fusion.3
  223.0 3.5 fusion.88
  231.6 26.5 %reduce-scatter.11.cloned.1.call-done = bf16[256,640]{1,0:T(8,128)(2,1)} async-done(((bf16[1024,640]{1,0:T(8,128)(2,1)}), bf16[256,640]{1,0:T(8,128)(2,1)}) %reduce-scatter.11.cloned.1.call-update) | async-done | bytes 327696 | tf_op jit(solution)/shard_map/reduce_scatter | solution.py:197
  263.3 18.1 %all-gather.16.cloned.1.call-done = bf16[1024,640]{1,0:T(8,128)(2,1)} async-done(((bf16[256,640]{1,0:T(8,128)(2,1)}), bf16[1024,640]{1,0:T(8,128)(2,1)}) %all-gather.16.cloned.1.call-update) | async-done | bytes 1310736 | tf_op jit(solution)/shard_map/all_gather | solution.py:205
  281.4 5.1 fusion.111
  288.6 2.9 convolution_convert_fusion.2
  291.6 26.7 %reduce-scatter.13.cloned.1.call-done = bf16[256,640]{1,0:T(8,128)(2,1)} async-done(((bf16[1024,640]{1,0:T(8,128)(2,1)}), bf16[256,640]{1,0:T(8,128)(2,1)}) %reduce-scatter.13.cloned.1.call-update) | async-done | bytes 327696 | tf_op jit(solution)/shard_map/reduce_scatter | solution.py:221
  321.1 3.1 fusion.117
  326.6 3.6 fusion.267
  331.6 12.5 %all-gather.18.cloned.1.call-done = bf16[1024,640]{1,0:T(8,128)(2,1)} async-done(((bf16[256,640]{1,0:T(8,128)(2,1)}), bf16[1024,640]{1,0:T(8,128)(2,1)}) %all-gather.18.cloned.1.call-update) | async-done | bytes 1310736 | tf_op jit(solution)/shard_map/all_gather | solution.py:227
  354.6 7.6 collective-permute-done.2
  365.8 4.2 fusion.174
  372.1 41.4 %reduce-scatter.23.cloned.1.call-done = f32[512,80]{0,1:T(8,128)} async-done(((f32[512,640]{0,1:T(8,128)}), f32[512,80]{0,1:T(8,128)}) %reduce-scatter.23.cloned.1.call-update) | async-done | bytes 163856 | tf_op jit(solution)/shard_map/reduce_scatter | solution.py:314
  415.1 42.6 %all_gather.67 = bf16[512,640]{0,1:T(8,128)(2,1)S(1)} all-gather(bf16[512,80]{0,1:T(8,128)(2,1)S(1)} %get-tuple-element.119), channel_id=1, replica_groups=mesh['dp'=8,'tensor'=4] {'dp'}, dimensions={1}, use_global_device_ids=true | all-gather | bytes 737280 | tf_op jit(solution)/shard_map/all_gather | solution.py:343
  460.2 4.3 fusion.87
  466.4 2.3 convolution_add_fusion.3
  468.7 2.7 fusion.284
  473.4 2.7 convolution_add_fusion.2
  476.1 2.7 fusion.285
  480.8 2.3 convolution_add_fusion.1
  484.1 2.7 fusion.286
  486.9 3.1 fusion.20
  495.7 3.3 convolution_add_fusion.6
  499.1 2.7 convolution_multiply_fusion.18
  505.1 2.5 fusion.159
  513.9 3.5 convolution_add_fusion
  517.4 3.6 fusion.287
  522.8 5.5 all-gather.1
  529.0 3.8 fusion.19
  535.9 7.1 psum.31
  545.5 15.9 %reduce-scatter.19.cloned.1.call-done = f32[256,80]{0,1:T(8,128)} async-done(((f32[256,640]{0,1:T(8,128)}), f32[256,80]{0,1:T(8,128)}) %reduce-scatter.19.cloned.1.call-update) | async-done | bytes 81936 | tf_op jit(solution)/shard_map/reduce_scatter | solution.py:312
  563.0 31.9 %all_gather.65 = bf16[256,640]{0,1:T(8,128)(2,1)S(1)} all-gather(bf16[256,80]{0,1:T(8,128)(2,1)S(1)} %get-tuple-element.123), channel_id=1, replica_groups=mesh['dp'=8,'tensor'=4] {'dp'}, dimensions={1}, use_global_device_ids=true | all-gather | bytes 368640 | tf_op jit(solution)/shard_map/all_gather | solution.py:337
  603.5 3.6 multiply_reduce_fusion
  614.7 34.8 %all-reduce.8 = f32[3072]{0:T(1024)S(1)} all-reduce(f32[3072]{0:T(1024)S(1)} %pad_maximum_fusion.25), channel_id=10, replica_groups=mesh['dp'=8,'tensor'=4] {'dp'}, use_global_device_ids=true, to_apply=%region_40.41.clone | all-reduce | flops 3072 | bytes 24576
  649.6 3.4 fusion.112
  655.9 31.5 %all_gather.63 = bf16[640,256]{1,0:T(8,128)(2,1)S(1)} all-gather(bf16[80,256]{1,0:T(8,128)(2,1)S(1)} %get-tuple-element.127), channel_id=1, replica_groups=mesh['dp'=8,'tensor'=4] {'dp'}, dimensions={0}, use_global_device_ids=true | all-gather | bytes 368640 | tf_op jit(solution)/shard_map/all_gather | solution.py:331
  705.9 2.7 fusion.42
  712.8 2.8 fusion.252
  717.5 3.1 fusion.50
  724.8 2.8 fusion.250
  729.6 2.5 fusion.249
  732.1 4.9 multiply_add_fusion.2
  737.0 2.7 fusion.282
  743.9 3.0 fusion.248
  748.8 2.3 fusion.247
  751.1 3.0 fusion.75
  756.1 2.7 fusion.280
  758.7 2.3 fusion.31
  763.4 2.8 fusion.246
  768.1 2.3 fusion.245
  770.4 3.2 fusion.74
  775.5 2.8 fusion.17
  778.4 2.8 fusion.18
  782.0 3.0 convert_element_type.219
  786.6 31.6 %all_gather.64 = bf16[640,512]{1,0:T(8,128)(2,1)S(1)} all-gather(bf16[80,512]{1,0:T(8,128)(2,1)S(1)} %get-tuple-element.125), channel_id=1, replica_groups=mesh['dp'=8,'tensor'=4] {'dp'}, dimensions={0}, use_global_device_ids=true | all-gather | bytes 737280 | tf_op jit(solution)/shard_map/all_gather | solution.py:334
  (500 shorter events, 186.4 us)
Async XLA Ops:
  8.0 31.5 %copy-start.64 = (f32[80,256]{1,0:T(8,128)S(1)}, f32[80,256]{1,0:T(8,128)}, u32[]{:S(2)}) copy-start(f32[80,256]{1,0:T(8,128)} %param.30) | copy-start | bytes 245764
  8.0 31.5 %copy-start.56 = (f32[80,512]{1,0:T(8,128)S(1)}, f32[80,512]{1,0:T(8,128)}, u32[]{:S(2)}) copy-start(f32[80,512]{1,0:T(8,128)} %param.31) | copy-start | bytes 491524
  8.0 173.0 %reduce-scatter.9.cloned.1.call-start = ((), (), s32[]{:S(2)}) async-start(), calls=%async_computation.8 | async-start | bytes 1638400 | tf_op jit(solution)/shard_map/reduce_scatter | solution.py:185
  8.8 93.2 %copy-start.7 = (bf16[1024,640]{1,0:T(8,128)(2,1)S(1)}, bf16[1024,640]{1,0:T(8,128)(2,1)}, u32[]{:S(2)}) copy-start(bf16[1024,640]{1,0:T(8,128)(2,1)} %param.27) | copy-start | bytes 3932164
  11.2 92.5 %copy-start.73 = (f32[1024]{0:T(1024)}, f32[1024]{0:T(1024)S(1)}, u32[]{:S(2)}) copy-start(f32[1024]{0:T(1024)S(1)} %fusion.197) | copy-start | bytes 12292
  39.5 64.2 %copy-start.88 = (f32[640]{0:T(1024)}, f32[640]{0:T(1024)S(1)}, u32[]{:S(2)}) copy-start(f32[640]{0:T(1024)S(1)} %get-tuple-element.159) | copy-start | bytes 7684
  70.4 33.3 %copy-start.27 = (bf16[640,256]{1,0:T(8,128)(2,1)}, bf16[640,256]{1,0:T(8,128)(2,1)S(1)}, u32[]{:S(2)}) copy-start(bf16[640,256]{1,0:T(8,128)(2,1)S(1)} %all_gather.52) | copy-start | bytes 983044
  102.1 5.9 copy-start.129
  105.6 45.3 %collective-permute-start.1 = (bf16[512,256]{0,1:T(8,128)(2,1)}, bf16[512,256]{0,1:T(8,128)(2,1)S(1)}, u32[]{:S(2)}, u32[]{:S(2)}) collective-permute-start(bf16[512,256]{0,1:T(8,128)(2,1)} %slice.321), channel_id=1, source_target_pairs={{0,4},{4,8},{8,12},{12,16},{16,20},{20,24},{24,28},{1,5},{5,9},{9,... | collective-permute-start | bytes 786440 | tf_op jit(solution)/shard_map/ppermute | solution.py:27
  112.1 37.2 %copy-start.32 = (bf16[1024,128]{0,1:T(8,128)(2,1)}, bf16[1024,128]{0,1:T(8,128)(2,1)S(1)}, u32[]{:S(2)}) copy-start(bf16[1024,128]{0,1:T(8,128)(2,1)S(1)} %get-tuple-element.151) | copy-start | bytes 786436
  112.1 37.2 %copy-start.34 = (bf16[1024,128]{0,1:T(8,128)(2,1)}, bf16[1024,128]{0,1:T(8,128)(2,1)S(1)}, u32[]{:S(2)}) copy-start(bf16[1024,128]{0,1:T(8,128)(2,1)S(1)} %get-tuple-element.152) | copy-start | bytes 786436
  112.1 37.2 %copy-start.49 = (bf16[1024,128]{0,1:T(8,128)(2,1)}, bf16[1024,128]{0,1:T(8,128)(2,1)S(1)}, u32[]{:S(2)}) copy-start(bf16[1024,128]{0,1:T(8,128)(2,1)S(1)} %get-tuple-element.173) | copy-start | bytes 786436
  112.2 37.2 %copy-start.51 = (bf16[1024,128]{0,1:T(8,128)(2,1)}, bf16[1024,128]{0,1:T(8,128)(2,1)S(1)}, u32[]{:S(2)}) copy-start(bf16[1024,128]{0,1:T(8,128)(2,1)S(1)} %get-tuple-element.174) | copy-start | bytes 786436
  112.2 37.1 %collective-permute-start = (bf16[512,256]{0,1:T(8,128)(2,1)S(1)}, bf16[512,256]{0,1:T(8,128)(2,1)S(1)}, u32[]{:S(2)}, u32[]{:S(2)}) collective-permute-start(bf16[512,256]{0,1:T(8,128)(2,1)S(1)} %pad_maximum_fusion.18), channel_id=1, source_target_pairs={{0,4},{4,8},{8,12},{12,16},{16,20},{20,24},{24,28},{1,5},{5,9},{9,... | collective-permute-start | bytes 786440 | tf_op jit(solution)/shard_map/ppermute | solution.py:27
  118.1 34.7 %copy-start.66 = (bf16[512,256]{1,0:T(8,128)(2,1)}, bf16[512,256]{1,0:T(8,128)(2,1)S(1)}, u32[]{:S(2)}) copy-start(bf16[512,256]{1,0:T(8,128)(2,1)S(1)} %convolution_convert_fusion.5) | copy-start | bytes 786436
  118.4 32.4 %copy-start.38 = (bf16[1024,256]{0,1:T(8,128)(2,1)}, bf16[1024,256]{0,1:T(8,128)(2,1)S(1)}, u32[]{:S(2)}) copy-start(bf16[1024,256]{0,1:T(8,128)(2,1)S(1)} %slice.322) | copy-start | bytes 1572868
  149.3 3.6 copy-start.44
  155.3 65.2 %all-gather.12.cloned.1.call-start = ((), (), s32[]{:S(2)}) async-start(), calls=%async_computation.10 | async-start | bytes 1474560 | tf_op jit(solution)/shard_map/all_gather | solution.py:100
  156.1 66.9 %all-gather.10.cloned.1.call-start = ((), (), s32[]{:S(2)}) async-start(), calls=%async_computation.9 | async-start | bytes 1638400 | tf_op jit(solution)/shard_map/all_gather | solution.py:191
  156.1 26.1 %copy-start.78 = (f32[640]{0:T(1024)S(1)}, f32[640]{0:T(1024)}, u32[]{:S(2)}) copy-start(f32[640]{0:T(1024)} %get-tuple-element.158) | copy-start | bytes 7684
  159.1 25.5 %copy-start.81 = (f32[640]{0:T(1024)S(1)}, f32[640]{0:T(1024)}, u32[]{:S(2)}) copy-start(f32[640]{0:T(1024)} %get-tuple-element.157) | copy-start | bytes 7684
  182.2 3.3 copy-start.109
  182.2 3.3 copy-start.101
  182.2 3.4 copy-start.58
  185.5 72.6 %reduce-scatter.11.cloned.1.call-start = ((), (), s32[]{:S(2)}) async-start(), calls=%async_computation.11 | async-start | bytes 1638400 | tf_op jit(solution)/shard_map/reduce_scatter | solution.py:197
  231.5 27.8 %copy-start.80 = (f32[640]{0:T(1024)S(1)}, f32[640]{0:T(1024)}, u32[]{:S(2)}) copy-start(f32[640]{0:T(1024)} %get-tuple-element.156) | copy-start | bytes 7684
  231.6 49.9 %all-gather.16.cloned.1.call-start = ((), (), s32[]{:S(2)}) async-start(), calls=%async_computation.13 | async-start | bytes 1638400 | tf_op jit(solution)/shard_map/all_gather | solution.py:205
  259.3 27.3 %copy-start.103 = (f32[256]{0:T(256)}, f32[256]{0:T(256)S(1)}, u32[]{:S(2)}) copy-start(f32[256]{0:T(256)S(1)} %fusion.202) | copy-start | bytes 3076
  263.3 55.0 %reduce-scatter.13.cloned.1.call-start = ((), (), s32[]{:S(2)}) async-start(), calls=%async_computation.14 | async-start | bytes 1638400 | tf_op jit(solution)/shard_map/reduce_scatter | solution.py:221
  281.4 7.2 copy-start.53
  281.4 7.2 copy-start.54
  291.5 29.5 %copy-start.21 = (bf16[256,640]{1,0:T(8,128)(2,1)S(1)}, bf16[256,640]{1,0:T(8,128)(2,1)}, u32[]{:S(2)}) copy-start(bf16[256,640]{1,0:T(8,128)(2,1)} %reduce-scatter.11.cloned.1.call-done) | copy-start | bytes 983044
  291.6 52.6 %all-gather.18.cloned.1.call-start = ((), (), s32[]{:S(2)}) async-start(), calls=%async_computation.15 | async-start | bytes 1638400 | tf_op jit(solution)/shard_map/all_gather | solution.py:227
  321.0 3.2 copy-start.110
  321.0 4.0 copy-start.22
  321.0 4.0 copy-start.79
  321.0 4.0 copy-start.102
  326.0 87.5 %reduce-scatter.23.cloned.1.call-start = ((), (), s32[]{:S(2)}) async-start(), calls=%async_computation.22 | async-start | bytes 1474560 | tf_op jit(solution)/shard_map/reduce_scatter | solution.py:314
  330.2 13.9 %copy-start.45 = (bf16[256,640]{0,1:T(8,128)(2,1)S(1)}, bf16[256,640]{0,1:T(8,128)(2,1)}, u32[]{:S(2)}) copy-start(bf16[256,640]{0,1:T(8,128)(2,1)} %copy-done.44) | copy-start | bytes 983044
  330.3 173.5 %all-reduce.13.cloned.1.call-start = ((), (), s32[]{:S(2)}) async-start(), calls=%async_computation.16 | async-start | bytes 1048576 | tf_op jit(solution)/shard_map/psum | solution.py:281
  346.2 5.2 copy-start.36
  350.1 12.1 %collective-permute-start.2 = (bf16[512,256]{0,1:T(8,128)(2,1)S(1)}, bf16[512,256]{0,1:T(8,128)(2,1)S(1)}, u32[]{:S(2)}, u32[]{:S(2)}) collective-permute-start(bf16[512,256]{0,1:T(8,128)(2,1)S(1)} %slice.492), channel_id=1, source_target_pairs={{4,0},{8,4},{12,8},{16,12},{20,16},{24,20},{28,24},{5,1},{9,5},{13... | collective-permute-start | bytes 786440 | tf_op jit(solution)/shard_map/ppermute | solution.py:27
  363.2 172.7 %all-gather.14.cloned.1.call-start = ((), (), s32[]{:S(2)}) async-start(), calls=%async_computation.12 | async-start | bytes 1638400 | tf_op jit(solution)/shard_map/all_gather | solution.py:204
  363.8 179.8 %reduce-scatter.21.cloned.1.call-start = ((), (), s32[]{:S(2)}) async-start(), calls=%async_computation.21 | async-start | bytes 2949120 | tf_op jit(solution)/shard_map/reduce_scatter | solution.py:313
  372.0 41.5 %copy-start.71 = (f32[512,80]{0,1:T(8,128)S(1)}, f32[512,80]{0,1:T(8,128)}, u32[]{:S(2)}) copy-start(f32[512,80]{0,1:T(8,128)} %param.40) | copy-start | bytes 491524
  372.0 189.4 %reduce-scatter.19.cloned.1.call-start = ((), (), s32[]{:S(2)}) async-start(), calls=%async_computation.20 | async-start | bytes 737280 | tf_op jit(solution)/shard_map/reduce_scatter | solution.py:312
  486.9 3.1 copy-start.4
  490.6 3.6 copy-start.20
  491.4 10.3 %collective-permute-start.3 = (bf16[512,256]{0,1:T(8,128)(2,1)}, bf16[512,256]{0,1:T(8,128)(2,1)}, u32[]{:S(2)}, u32[]{:S(2)}) collective-permute-start(bf16[512,256]{0,1:T(8,128)(2,1)} %slice.491), channel_id=1, source_target_pairs={{4,0},{8,4},{12,8},{16,12},{20,16},{24,20},{28,24},{5,1},{9,5},{13... | collective-permute-start | bytes 786440 | tf_op jit(solution)/shard_map/ppermute | solution.py:27
  499.0 104.4 %all-reduce.15.cloned.1.call-start = ((), (), s32[]{:S(2)}) async-start(), calls=%async_computation.24 | async-start | bytes 3670016 | tf_op jit(solution)/shard_map/psum | solution.py:282
  512.6 141.7 %reduce-scatter.15.cloned.1.call-start = ((), (), s32[]{:S(2)}) async-start(), calls=%async_computation.18 | async-start | bytes 737280 | tf_op jit(solution)/shard_map/reduce_scatter | solution.py:310
  517.4 3.7 copy-start.8
  517.4 3.7 copy-start.40
  517.4 3.7 copy-start.89
  522.7 178.7 %all-gather.22.cloned.1.call-start = ((), (), s32[]{:S(2)}) async-start(), calls=%async_computation.23 | async-start | bytes 1474560 | tf_op jit(solution)/shard_map/all_gather | solution.py:340
  532.9 10.7 %copy-start.63 = (f32[2,80,512]{2,1,0:T(8,128)S(1)}, f32[2,80,512]{2,1,0:T(8,128)}, u32[]{:S(2)}) copy-start(f32[2,80,512]{2,1,0:T(8,128)} %param.39) | copy-start | bytes 983044
  535.2 26.2 %copy-start.76 = (f32[256,80]{0,1:T(8,128)S(1)}, f32[256,80]{0,1:T(8,128)}, u32[]{:S(2)}) copy-start(f32[256,80]{0,1:T(8,128)} %param.38) | copy-start | bytes 245764
  545.4 236.5 %all-gather.20.cloned.1.call-start = ((), (), s32[]{:S(2)}) async-start(), calls=%async_computation.17 | async-start | bytes 1638400 | tf_op jit(solution)/shard_map/all_gather | solution.py:295
  603.5 3.7 copy-start.92
  603.5 3.8 copy-start.19
  603.5 3.7 copy-start.122
  609.3 175.7 %reduce-scatter.17.cloned.1.call-start = ((), (), s32[]{:S(2)}) async-start(), calls=%async_computation.19 | async-start | bytes 1474560 | tf_op jit(solution)/shard_map/reduce_scatter | solution.py:311
  703.2 26.4 %copy-start.13 = (f32[2,640,512]{2,1,0:T(8,128)}, f32[2,640,512]{2,1,0:T(8,128)S(1)}, u32[]{:S(2)}) copy-start(f32[2,640,512]{2,1,0:T(8,128)S(1)} %convert_element_type.229) | copy-start | bytes 7864324
  818.4 11.2 %copy-start.9 = (f32[640,512]{1,0:T(8,128)}, f32[640,512]{1,0:T(8,128)S(1)}, u32[]{:S(2)}) copy-start(f32[640,512]{1,0:T(8,128)S(1)} %convert_element_type.225) | copy-start | bytes 3932164
  (90 other events, 153.8 us)
Sparse Core Ops, SparseCore 0:
  155.4 25.5 reduce-scatter.8
  231.7 26.4 reduce-scatter.10
  291.7 26.5 reduce-scatter.12
  363.4 34.7 all-reduce.12
  400.2 18.2 all-gather.13
  512.7 47.5 all-reduce.14
Sparse Core Ops, SparseCore 1:
  158.8 44.3 all-gather.11
  205.2 17.6 all-gather.9
  263.4 18.0 all-gather.15
  326.1 18.0 all-gather.17
  348.5 64.9 reduce-scatter.22
  418.0 73.4 reduce-scatter.20
  499.1 62.3 reduce-scatter.18
  565.1 61.3 reduce-scatter.14
  629.4 42.8 all-gather.21
  673.9 16.7 all-gather.19
  694.9 64.4 reduce-scatter.16
where the time goes:
time: 865 us; the launch traced here: 856 us
  blocking collectives  341 us (39%)
  matrix products  218 us (25%)
  waiting for transfers between devices  172 us (20%)
  other arithmetic  66 us (8%)
  local copies, waits for them, and re-layouts  26.9 us (3%)
  between operations  24.3 us (3%)
    dot_general x35, matrix products, orthogonalize(): square = jnp.dot(current, current.T, precision=HIGHEST)  70.2 us
    dot_general x35, matrix products, orthogonalize(): jnp.dot(polynomial, current, precision=HIGHEST)  55 us
    all_gather x1, blocking collectives, shards(): lax.all_gather(nest_down.astype(jnp.bfloat16), 'dp', axis=1, tiled=True)  42.6 us
    reduce_scatter x1, waiting for transfers between devices, shards(): lax.psum_scatter(grad_down_local, 'dp', scatter_dimension=1, tiled=True)  41.4 us
    dot_general x35, matrix products, orthogonalize(): jnp.dot(square, square, precision=HIGHEST)  39.6 us
    all_gather x1, blocking collectives, shards(): lax.all_gather(w_down.astype(low_type), 'dp', axis=1, tiled=True)  34.9 us
    unnamed x1, blocking collectives  34.8 us
    all_gather x1, blocking collectives, shards(): lax.all_gather(nest_out.astype(jnp.bfloat16), 'dp', axis=1, tiled=True)  31.9 us
  transfers between devices with their start and end apart: 21, of which 8 were waited for; matrix products, arithmetic and copies ran while one was open for 27% of the time, Pallas kernels for 0%

commit v1 on v0

v1 whole, which is shorter than its diff:
```python
import math

import jax
import jax.numpy as jnp
from jax import lax
from jax.experimental import pallas as pl
from jax.experimental.pallas import tpu as pltpu
from jax.sharding import PartitionSpec as P

WINDOW = 512
NS_ITERS = 5


EPSILON = 1e-06
MOMENTUM = 0.95
MUON_RATE = 0.5
ROPE_BASE = 10000.0
COEF_FIRST = 3.4445
COEF_SECOND = -4.775
COEF_THIRD = 2.0315
MASKED = -1e30
LANES = 128


def from_behind(block, axis, distance):
    devices = range(lax.axis_size(axis))
    route = [(i - distance, i) for i in devices if i - distance in devices]
    return lax.ppermute(block, axis, route)


def rms_scale(values, scale_gain):
    inverse = lax.rsqrt(jnp.mean(values * values, axis=-1, keepdims=True) + EPSILON)
    return values * inverse * (1.0 + scale_gain)


def rotate(values, position):
    half_dim = values.shape[-1] // 2
    exponent = jnp.arange(half_dim).astype(jnp.float32) * (-2.0 / values.shape[-1])
    frequency = jnp.power(ROPE_BASE, exponent)
    angles = position.astype(jnp.float32)[:, None] * frequency[None, :]
    cosine = jnp.cos(angles)
    sine_vals = jnp.sin(angles)
    first_half = values[..., :half_dim]
    second_half = values[..., half_dim:]
    return jnp.concatenate(
        [
            first_half * cosine - second_half * sine_vals,
            second_half * cosine + first_half * sine_vals,
        ],
        axis=-1,
    )


def sweep_kernel(start_ref, block_ref, result_ref):
    low_type = jnp.bfloat16
    full_type = jnp.float32

    def halves(values):
        high = values.astype(low_type)
        return high, (values - high.astype(full_type)).astype(low_type)

    def product(left, right):
        left_high, left_low = left
        right_high, right_low = right
        total = jnp.dot(left_high, right_high, preferred_element_type=full_type)
        total += jnp.dot(left_high, right_low, preferred_element_type=full_type)
        return total + jnp.dot(left_low, right_high, preferred_element_type=full_type)

    result_ref[...] = start_ref[...]

    @pl.loop(0, NS_ITERS)
    def _(sweep_index):
        current = result_ref[...]
        current_halves = halves(current)
        square = block_ref[...] * lax.dot_general(
            current_halves[0],
            current_halves[0],
            (((1,), (1,)), ((), ())),
            preferred_element_type=full_type,
        )
        square_halves = halves(square)
        polynomial = COEF_SECOND * square + COEF_THIRD * product(square_halves, square_halves)
        result_ref[...] = COEF_FIRST * current + product(halves(polynomial), current_halves)


def orthogonalize(matrix, paired):
    rows = matrix.shape[0]
    half = rows // 2
    row_sums = jnp.sum(matrix * matrix, axis=1)
    upper, lower = jnp.sum(row_sums[:half]), jnp.sum(row_sums[half:])
    own_half = jnp.arange(rows) < half
    sums = jnp.where(paired, jnp.where(own_half, upper, lower), upper + lower)
    start = matrix / (jnp.sqrt(sums) + 1e-07)[:, None]
    same = own_half[:, None] == own_half[None, :]
    block = jnp.where(paired, same.astype(jnp.float32), 1.0)
    return pl.pallas_call(
        sweep_kernel,
        out_shape=jax.ShapeDtypeStruct(matrix.shape, jnp.float32),
        in_specs=[pl.BlockSpec(memory_space=pltpu.VMEM)] * 2,
        out_specs=pl.BlockSpec(memory_space=pltpu.VMEM),
        compiler_params=pltpu.CompilerParams(vmem_limit_bytes=40 * 1024 * 1024),
    )(start, block)


def shards(
    inputs,
    cotangent,
    seq_lengths,
    w_query,
    w_kv,
    w_out,
    w_gate_up,
    w_down,
    gains,
    mom_query,
    mom_kv,
    mom_out,
    mom_gate_up,
    mom_down,
    mom_gains,
):
    low_type = jnp.bfloat16
    full_type = jnp.float32
    row_count, width = inputs.shape
    head_dim = w_kv.shape[1] // 2
    hidden = w_down.shape[0]
    shard_rows = w_query.shape[0]
    dp_count = lax.axis_size("dp")
    dp_index = lax.axis_index("dp")
    tensor_count = lax.axis_size("tensor")
    tensor_index = lax.axis_index("tensor")
    own_rows = row_count // tensor_count
    window_rows = own_rows + WINDOW
    quarter = 2 * head_dim // tensor_count
    gain_size = gains.shape[0]
    gain_rows = -(-gain_size // LANES)
    score_scale = head_dim ** (-0.5)
    task_width = hidden
    matrix_width = 4 * task_width
    both = ("tensor", "dp")

    def ein(form, left, right):
        return jnp.einsum(form, left, right, preferred_element_type=full_type)

    def pack_gains(values):
        padded = jnp.pad(values, (0, gain_rows * LANES - gain_size)).reshape(gain_rows, LANES)
        return jnp.pad(padded, ((0, shard_rows - gain_rows), (0, 0)))

    halo = from_behind(inputs[row_count - WINDOW :], "dp", 1)
    kv_quarter = lax.dynamic_slice_in_dim(w_kv, tensor_index * quarter, quarter, 1)
    packed = jnp.concatenate(
        [w_query, w_out.T, w_gate_up[0], w_gate_up[1], w_down.T, kv_quarter, pack_gains(gains)],
        axis=1,
    ).astype(low_type)
    whole = lax.all_gather(packed, both, axis=0, tiled=True)
    whole = whole.reshape(tensor_count, width, packed.shape[1])
    query_weight = whole[:, :, :head_dim]
    out_weight = whole[:, :, head_dim : 2 * head_dim]
    gate_weight = whole[:, :, task_width : 2 * task_width]
    up_weight = whole[:, :, 2 * task_width : 3 * task_width]
    down_weight = whole[:, :, 3 * task_width : matrix_width]
    kv_weight = whole[:, :, matrix_width : matrix_width + quarter]
    kv_weight = kv_weight.transpose(1, 0, 2).reshape(width, 2 * head_dim)
    gain_vals = whole[0, :, matrix_width + quarter :].reshape(dp_count, shard_rows * LANES)
    gain_vals = gain_vals[:, :gain_size].reshape(-1).astype(full_type)
    gain_in = gain_vals[0:width]
    gain_attn = gain_vals[width : 2 * width]
    gain_pre = gain_vals[2 * width : 3 * width]
    gain_post = gain_vals[3 * width : 4 * width]
    gain_query = gain_vals[4 * width : 4 * width + head_dim]
    gain_key = gain_vals[4 * width + head_dim :]

    first_row = tensor_index * own_rows
    places = dp_index * row_count + first_row - WINDOW
    places = places + jnp.arange(window_rows, dtype=jnp.int32)
    seq_ends = jnp.cumsum(seq_lengths)
    passed = places[:, None] >= seq_ends[None, :]
    segment = jnp.sum(passed.astype(jnp.int32), axis=1)
    seq_starts = jnp.sum(jnp.where(passed, seq_lengths[None, :], 0), axis=1)
    segment = jnp.where(places < 0, -1, segment)
    position = places - seq_starts
    gap = places[WINDOW:, None] - places[None, :]
    allowed = (segment[WINDOW:, None] == segment[None, :]) & (gap >= 0) & (gap < WINDOW)
    allowed = jnp.broadcast_to(allowed[None], (tensor_count, own_rows, window_rows))
    allowed = allowed.reshape(tensor_count * own_rows, window_rows)

    def query_map(raw, scale_gain):
        flat = raw.reshape(tensor_count * own_rows, head_dim)
        return rotate(rms_scale(flat, scale_gain), jnp.tile(position[WINDOW:], tensor_count))

    def key_map(raw, scale_gain):
        return rotate(rms_scale(raw, scale_gain), position)

    def activate(gate_raw, up_raw):
        return jax.nn.gelu(gate_raw, approximate=True) * up_raw

    extended = jnp.concatenate([halo, inputs], axis=0)
    window_in = lax.dynamic_slice_in_dim(extended, first_row, window_rows, 0).astype(full_type)
    own_in = window_in[WINDOW:]
    back_out = lax.dynamic_slice_in_dim(cotangent, first_row, own_rows, 0).astype(full_type)
    normed_f, input_norm_back = jax.vjp(rms_scale, window_in, gain_in)
    normed_window = normed_f.astype(low_type)
    normed = normed_window[WINDOW:]
    query_raw = ein("td,hdc->htc", normed, query_weight)
    kv_raw = ein("td,dc->tc", normed_window, kv_weight)
    queries_f, query_back = jax.vjp(query_map, query_raw, gain_query)
    keys_f, key_back = jax.vjp(key_map, kv_raw[:, :head_dim], gain_key)
    queries = queries_f.astype(low_type)
    key_rows = keys_f.astype(low_type)
    value_rows = kv_raw[:, head_dim:].astype(low_type)
    scores = ein("qd,kd->qk", queries, key_rows) * score_scale
    scores = jnp.where(allowed, scores, MASKED)
    weights = jnp.exp(scores - jnp.max(scores, axis=1, keepdims=True))
    probs = weights / jnp.sum(weights, axis=1, keepdims=True)
    probs_low = probs.astype(low_type)
    attended = ein("qk,kd->qd", probs_low, value_rows).astype(low_type)
    attended = attended.reshape(tensor_count, own_rows, head_dim)
    attn_raw = ein("htc,hdc->td", attended, out_weight)
    branch_attn, attn_norm_back = jax.vjp(rms_scale, attn_raw, gain_attn)
    hidden_rows = own_in + branch_attn
    ffn_f, pre_norm_back = jax.vjp(rms_scale, hidden_rows, gain_pre)
    ffn_in = ffn_f.astype(low_type)
    gate = ein("td,hdf->htf", ffn_in, gate_weight)
    up = ein("td,hdf->htf", ffn_in, up_weight)
    mixed_f, activate_back = jax.vjp(activate, gate, up)
    mixed = mixed_f.astype(low_type)
    down_raw = ein("htf,hdf->td", mixed, down_weight)
    branch_ffn, post_norm_back = jax.vjp(rms_scale, down_raw, gain_post)
    output_own = (hidden_rows + branch_ffn).astype(low_type)
    output = lax.all_gather(output_own, "tensor", axis=0, tiled=True)

    back_down_f, grad_gain_post = post_norm_back(back_out)
    back_down = back_down_f.astype(low_type)
    grad_down = ein("td,htf->hdf", back_down, mixed)
    back_gate_f, back_up_f = activate_back(ein("td,hdf->htf", back_down, down_weight))
    back_gate = back_gate_f.astype(low_type)
    back_up = back_up_f.astype(low_type)
    grad_gate = ein("td,htf->hdf", ffn_in, back_gate)
    grad_up = ein("td,htf->hdf", ffn_in, back_up)
    back_ffn = ein("htf,hdf->td", back_gate, gate_weight) + ein(
        "htf,hdf->td", back_up, up_weight
    )
    back_pre, grad_gain_pre = pre_norm_back(back_ffn)
    back_hidden = back_out + back_pre
    back_attn_f, grad_gain_attn = attn_norm_back(back_hidden)
    back_attn = back_attn_f.astype(low_type)
    grad_out = ein("td,htc->hdc", back_attn, attended)
    back_attended = ein("td,hdc->htc", back_attn, out_weight).astype(low_type)
    back_attended = back_attended.reshape(tensor_count * own_rows, head_dim)
    back_probs = ein("qd,kd->qk", back_attended, value_rows)
    row_dot = jnp.sum(probs * back_probs, axis=1, keepdims=True)
    back_scores = (probs * (back_probs - row_dot)).astype(low_type)
    back_queries = ein("qk,kd->qd", back_scores, key_rows) * score_scale
    back_keys = ein("qk,qd->kd", back_scores, queries) * score_scale
    back_values = ein("qk,qd->kd", probs_low, back_attended)
    back_query_raw_f, grad_gain_query = query_back(back_queries)
    back_query_raw = back_query_raw_f.astype(low_type)
    back_key_raw, grad_gain_key = key_back(back_keys)
    back_kv = jnp.concatenate([back_key_raw, back_values], axis=1).astype(low_type)
    grad_query = ein("td,htc->hdc", normed, back_query_raw)
    grad_kv = ein("td,tc->dc", normed_window, back_kv)
    back_normed = ein("tc,dc->td", back_kv, kv_weight)
    back_normed = back_normed.at[WINDOW:].add(ein("htc,hdc->td", back_query_raw, query_weight))
    back_in, grad_gain_in = input_norm_back(back_normed)

    grad_gains = jnp.concatenate(
        [grad_gain_in, grad_gain_attn, grad_gain_pre, grad_gain_post, grad_gain_query, grad_gain_key]
    )
    gain_block = jax.vmap(pack_gains)(grad_gains.reshape(dp_count, gain_size))
    gain_block = gain_block.reshape(1, width, LANES) * (1.0 / tensor_count)
    gain_block = jnp.broadcast_to(gain_block, (tensor_count, width, LANES))
    kv_parts = grad_kv.reshape(width, tensor_count, quarter).transpose(1, 0, 2)
    grads = jnp.concatenate(
        [grad_query, grad_out, grad_gate, grad_up, grad_down, kv_parts, gain_block], axis=2
    ).astype(low_type)
    summed = lax.psum_scatter(
        grads.reshape(tensor_count * width, grads.shape[2]), both, scatter_dimension=0, tiled=True
    ).astype(full_type)
    shared = lax.all_gather(summed[:, matrix_width:], "tensor", axis=0)
    grad_query = summed[:, :head_dim]
    grad_out = summed[:, head_dim : 2 * head_dim].T
    grad_gate_up = jnp.stack(
        [summed[:, task_width : 2 * task_width], summed[:, 2 * task_width : 3 * task_width]]
    )
    grad_down = summed[:, 3 * task_width : matrix_width].T
    grad_kv = shared[:, :, :quarter].transpose(1, 0, 2).reshape(shard_rows, 2 * head_dim)
    grad_gains = jnp.sum(shared[:, :gain_rows, quarter:], axis=0).reshape(-1)[:gain_size]

    spread = jnp.zeros((row_count + WINDOW, width), full_type)
    spread = lax.dynamic_update_slice_in_dim(
        spread, back_in.at[WINDOW:].add(back_hidden), first_row, 0
    )
    spread = lax.psum(spread.astype(low_type), "tensor")
    behind = from_behind(spread[:WINDOW], "dp", -1).astype(full_type)
    grad_input = spread[WINDOW:].astype(full_type).at[row_count - WINDOW :].add(behind)

    new_mom_query = MOMENTUM * mom_query + grad_query
    new_mom_kv = MOMENTUM * mom_kv + grad_kv
    new_mom_out = MOMENTUM * mom_out + grad_out
    new_mom_gate_up = MOMENTUM * mom_gate_up + grad_gate_up
    new_mom_down = MOMENTUM * mom_down + grad_down
    new_mom_gains = MOMENTUM * mom_gains + grad_gains
    nest_query = grad_query + MOMENTUM * new_mom_query
    nest_kv = grad_kv + MOMENTUM * new_mom_kv
    nest_out = grad_out + MOMENTUM * new_mom_out
    nest_gate_up = grad_gate_up + MOMENTUM * new_mom_gate_up
    nest_down = grad_down + MOMENTUM * new_mom_down
    nest_gains = grad_gains + MOMENTUM * new_mom_gains
    new_gains = gains - 0.1 / math.sqrt(row_count * dp_count) * nest_gains
    tasks = jnp.stack(
        [
            jnp.concatenate([nest_query, nest_out.T], axis=1),
            nest_gate_up[0],
            nest_gate_up[1],
            nest_down.T,
            nest_kv,
        ]
    ).astype(low_type)
    task_count = tasks.shape[0]
    tasks = jnp.pad(tasks, ((0, dp_count - task_count), (0, 0), (0, 0)))
    mine = lax.all_to_all(tasks, "dp", split_axis=0, concat_axis=0, tiled=True)
    mine = mine.reshape(width, task_width).T.astype(full_type)
    paired = (dp_index == 0) | (dp_index == 4)
    steps = orthogonalize(mine, paired).T.astype(low_type).reshape(dp_count, shard_rows, task_width)
    steps = lax.all_to_all(steps, "dp", split_axis=0, concat_axis=0, tiled=True)
    steps = steps.astype(full_type)

    def rate(rows, columns):
        return MUON_RATE * math.sqrt(max(1.0, rows / columns))

    new_query = w_query - rate(width, head_dim) * steps[0][:, :head_dim]
    new_out = w_out - rate(head_dim, width) * steps[0][:, head_dim:].T
    new_gate_up = w_gate_up - rate(width, hidden) * steps[1:3]
    new_down = w_down - rate(hidden, width) * steps[3].T
    new_kv = w_kv - rate(width, head_dim) * steps[4]
    return (
        output,
        grad_input,
        grad_query,
        grad_kv,
        grad_out,
        grad_gate_up,
        grad_down,
        grad_gains,
        new_query,
        new_kv,
        new_out,
        new_gate_up,
        new_down,
        new_gains,
        new_mom_query,
        new_mom_kv,
        new_mom_out,
        new_mom_gate_up,
        new_mom_down,
        new_mom_gains,
    )


def solution(mesh):
    return jax.shard_map(
        shards,
        mesh=mesh,
        in_specs=(
            P("dp", None),
            P("dp", None),
            P(),
            P("dp", "tensor"),
            P("dp", None),
            P("tensor", "dp"),
            P(None, "dp", "tensor"),
            P("tensor", "dp"),
            P("dp"),
            P("dp", "tensor"),
            P("dp", None),
            P("tensor", "dp"),
            P(None, "dp", "tensor"),
            P("tensor", "dp"),
            P("dp"),
        ),
        out_specs=(
            P("dp", None),
            P("dp", None),
            P("dp", "tensor"),
            P("dp", None),
            P("tensor", "dp"),
            P(None, "dp", "tensor"),
            P("tensor", "dp"),
            P("dp"),
            P("dp", "tensor"),
            P("dp", None),
            P("tensor", "dp"),
            P(None, "dp", "tensor"),
            P("tensor", "dp"),
            P("dp"),
            P("dp", "tensor"),
            P("dp", None),
            P("tensor", "dp"),
            P(None, "dp", "tensor"),
            P("tensor", "dp"),
            P("dp"),
        ),
        check_vma=False,
    )
```

time: 865 us -> 485 us (0.56)
  blocking collectives: 341 us -> 6.08 us
  matrix products: 218 us -> 30.6 us
  waiting for transfers between devices: 172 us -> 296 us
  local copies, waits for them, and re-layouts: 26.9 us -> 53.3 us
  other arithmetic: 66 us -> 44.4 us
  Pallas kernels: 0 us -> 14.3 us
  starting transfers between devices: 7.93 us -> 19 us
    all_gather x10 -> x1, blocking collectives: 299 us -> 6.08 us  [shards(): shared = lax.all_gather(summed[:, matrix_width:], 'tensor', axis=0)]
    dot_general x131 -> x24, matrix products: 218 us -> 30.6 us  [ein(): return jnp.einsum(form, left, right, preferred_element_type=full_type)]
    psum x2 -> x1, waiting for transfers between devices: 0.02 us -> 50.5 us  [shards(): spread = lax.psum(spread.astype(low_type), 'tensor')]
    all_gather x7 -> x2, waiting for transfers between devices: 30.6 us -> 74.1 us  [the longest x1 74.1 us: shards(): whole = lax.all_gather(packed, both, axis=0, tiled=True)]
    unnamed x1 -> x0, blocking collectives: 34.8 us -> none
    transpose x0 -> x8, local copies, waits for them, and re-layouts: none -> 21.7 us  [the longest x5 18 us: ein(): return jnp.einsum(form, left, right, preferred_element_type=full_type)]
    convert_element_type x27 -> x15, other arithmetic: 28.5 us -> 8.3 us  [the longest x1 1.49 us: shards(): spread[WINDOW:].astype(full_type).at[row_count - WINDOW:].add(behind)]
    pallas_call x0 -> x1, Pallas kernels: none -> 14.3 us  [orthogonalize(): pl.pallas_call(sweep_kernel, out_shape=jax.ShapeDtypeStruct(matrix.shape,...]
  transfers between devices with their start and end apart: 21 -> 8, of which waited for: 8 -> 5; matrix products, arithmetic and copies ran while one was open for 27% -> 5% of each run, Pallas kernels for 0% -> 3%
where the time goes in v1:
time: 485 us; the launch traced here: 480 us
  waiting for transfers between devices  296 us (61%)
  local copies, waits for them, and re-layouts  53.3 us (11%)
  other arithmetic  44.4 us (9%)
  matrix products  30.6 us (6%)
  starting transfers between devices  19 us (4%)
  between operations  16.2 us (3%)
  Pallas kernels  14.3 us (3%)
  blocking collectives  6.08 us (1%)
    reduce_scatter x1, waiting for transfers between devices, shards(): lax.psum_scatter(grads.reshape(tensor_count * width, grads.shape[2]), bot...  145 us
    all_gather x1, waiting for transfers between devices, shards(): whole = lax.all_gather(packed, both, axis=0, tiled=True)  74.1 us
    psum x1, waiting for transfers between devices, shards(): spread = lax.psum(spread.astype(low_type), 'tensor')  50.5 us
    dot_general x24, matrix products, ein(): return jnp.einsum(form, left, right, preferred_element_type=full_type)  30.6 us
    unnamed x84, local copies, waits for them, and re-layouts  21.5 us
    transpose x5, local copies, waits for them, and re-layouts, ein(): return jnp.einsum(form, left, right, preferred_element_type=full_type)  18 us
    pallas_call x1, Pallas kernels, orthogonalize(): pl.pallas_call(sweep_kernel, out_shape=jax.ShapeDtypeStruct(matrix.shape,...  14.3 us
    ppermute x2, waiting for transfers between devices, from_behind(): return lax.ppermute(block, axis, route)  14 us
  transfers between devices with their start and end apart: 8, of which 5 were waited for; matrix products, arithmetic and copies ran while one was open for 5% of the time, Pallas kernels for 3%

profile of v1, /device:TPU:0, one launch (start us, length us, event | category | flops | bytes accessed | tf_op | source)
XLA Modules:
  0.0 480.2 jit_solution(11471791390101839054)
XLA Ops:
  7.3 1.0 convert_dynamic-update-slice_fusion
  8.2 1.0 convert.110
  13.5 5.7 %collective-permute-start = (bf16[512,640]{1,0:T(8,128)(2,1)S(1)}, bf16[512,640]{1,0:T(8,128)(2,1)}, u32[]{:S(2)}, u32[]{:S(2)}) collective-permute-start(bf16[512,640]{1,0:T(8,128)(2,1)S(1)} %slice.202), channel_id=1, source_target_pairs={{0,4},{4,8},{8,12},{12,16},{16,20},{20,24},{24,28},{1,5},{5,9},{9,... | collective-permute-start | bytes 1966088 | tf_op jit(solution)/shard_map/ppermute | solution.py:28
  21.0 14.0 %collective-permute-done = bf16[512,640]{1,0:T(8,128)(2,1)} collective-permute-done((bf16[512,640]{1,0:T(8,128)(2,1)S(1)}, bf16[512,640]{1,0:T(8,128)(2,1)}, u32[]{:S(2)}, u32[]{:S(2)}) %collective-permute-start) | collective-permute-done | bytes 655392 | tf_op jit(solution)/shard_map/ppermute | solution.py:28
  34.9 1.6 multiply_reduce_fusion.3
  36.5 1.4 convert_element_type.133
  37.9 74.1 %all-gather.4.cloned.1.call-done = bf16[2560,2304]{1,0:T(8,128)(2,1)} async-done(((bf16[80,2304]{1,0:T(8,128)(2,1)}), bf16[2560,2304]{1,0:T(8,128)(2,1)}) %all-gather.4.cloned.1.call-update) | async-done | bytes 11796496 | tf_op jit(solution)/shard_map/all_gather | solution.py:155
  112.9 1.1 slice_bitcast_fusion
  114.8 2.0 fusion.53
  117.9 2.2 fusion.95
  120.3 2.4 fusion.88
  124.9 1.5 slice-done.1
  126.3 1.0 slice-done.2
  128.0 1.4 multiply_reduce_fusion.14
  129.5 1.1 fusion.12
  130.6 1.3 fusion.22
  131.9 1.1 multiply_reduce_fusion.13
  133.5 1.0 fusion.102
  134.6 2.5 fusion.21
  137.1 1.0 fusion.32
  138.1 1.2 multiply_reduce_fusion.9
  144.5 1.7 fusion.26
  146.1 2.5 convert_bitcast_fusion.2
  148.6 2.6 convert_bitcast_fusion.1
  151.2 2.4 convert_bitcast_fusion
  153.6 1.8 fusion.98
  157.4 1.6 convolution_convert_fusion.2
  159.0 2.3 fusion.91
  162.1 1.7 fusion.25
  165.2 2.4 copy.73
  167.6 2.6 constant_dynamic-update-slice_fusion.9
  170.2 2.4 copy.75
  172.7 4.4 copy.76
  177.1 4.4 copy.77
  181.4 4.4 copy.78
  185.8 2.2 copy.79
  188.1 2.7 constant_dynamic-update-slice_fusion.8
  190.9 1.8 constant_dynamic-update-slice_fusion.7
  193.5 1.7 constant_dynamic-update-slice_fusion.6
  195.3 0.9 copy-done.1
  196.2 1.7 constant_dynamic-update-slice_fusion.5
  198.0 1.0 constant_dynamic-update-slice_fusion.4
  199.0 0.9 constant_dynamic-update-slice_fusion.3
  200.0 1.7 add_add_fusion
  201.7 144.7 %reduce-scatter.2.cloned.1.call-done = bf16[80,2304]{1,0:T(8,128)(2,1)} async-done(((bf16[2560,2304]{1,0:T(8,128)(2,1)}), bf16[80,2304]{1,0:T(8,128)(2,1)}) %reduce-scatter.2.cloned.1.call-update) | async-done | bytes 368656 | tf_op jit(solution)/shard_map/reduce_scatter | solution.py:276
  346.4 1.5 add_convert_fusion.5
  347.9 6.1 %all-gather = f32[320,256]{1,0:T(8,128)S(1)} all-gather(f32[80,256]{1,0:T(8,128)S(1)} %get-tuple-element.110), channel_id=2, replica_groups=mesh['dp'=8,'tensor'=4] {'tensor'}, dimensions={0}, use_global_device_ids=true | all-gather | bytes 409600 | tf_op jit(solution)/shard_map/all_gather | solution.py:279
  354.8 1.1 convert_element_type.160
  359.9 4.4 all-to-all-start
  364.5 1.4 broadcast_in_dim.58
  365.9 1.0 constant_dynamic-update-slice_fusion.15
  367.6 50.5 %all-reduce.9.cloned.1.call-done = bf16[1536,640]{1,0:T(8,128)(2,1)} async-done(((bf16[1536,640]{1,0:T(8,128)(2,1)}), bf16[1536,640]{1,0:T(8,128)(2,1)}) %all-reduce.9.cloned.1.call-update) | async-done | bytes 1966096 | tf_op jit(solution)/shard_map/psum | solution.py:293
  418.1 2.0 slice.279
  420.0 1.3 collective-permute-start.1
  421.3 1.3 bitcast_convert_fusion
  422.6 1.7 copy.81
  426.5 1.3 sqrt_add_fusion
  427.9 14.3 %shard_map.302 = f32[512,640]{1,0:T(8,128)S(1)} custom-call(f32[512,640]{1,0:T(8,128)S(1)} %divide_bitcast_fusion.start_ref, f32[512,512]{1,0:T(8,128)S(1)} %convert_select_fusion.block_ref), custom_call_target="tpu_custom_call" | custom-call | tf_op jit(solution)/shard_map/pallas_call | solution.py:96
  442.3 1.1 copy.82
  443.4 7.5 %all-to-all-start.1 = ((bf16[8,80,512]{2,1,0:T(8,128)(2,1)}), bf16[8,80,512]{2,1,0:T(8,128)(2,1)S(1)}, u32[]{:S(2)}, u32[]{:S(2)}) async-start(bf16[8,80,512]{2,1,0:T(8,128)(2,1)} %bitcast.61), calls=%async_computation.2 | async-start | bytes 1310720 | tf_op jit(solution)/shard_map/all_to_all | solution.py:325
  451.0 1.5 slice_convert_fusion
  452.5 1.3 fusion.31
  455.3 12.6 %all-to-all-done.1 = bf16[8,80,512]{2,1,0:T(8,128)(2,1)S(1)} async-done(((bf16[8,80,512]{2,1,0:T(8,128)(2,1)}), bf16[8,80,512]{2,1,0:T(8,128)(2,1)S(1)}, u32[]{:S(2)}, u32[]{:S(2)}) %all-to-all-start.1) | async-done | bytes 655392 | tf_op jit(solution)/shard_map/all_to_all | solution.py:325
  472.3 1.1 copy.122
  (176 shorter events, 35.0 us)
Async XLA Ops:
  7.2 6.2 %copy-start.9 = (bf16[1024,640]{1,0:T(8,128)(2,1)S(1)}, bf16[1024,640]{1,0:T(8,128)(2,1)}, u32[]{:S(2)}) copy-start(bf16[1024,640]{1,0:T(8,128)(2,1)} %param.21) | copy-start | bytes 3932164
  7.2 12.0 %copy-start.28 = (s32[3]{0:T(128)S(1)}, s32[3]{0:T(128)}, u32[]{:S(2)}) copy-start(s32[3]{0:T(128)} %param.23) | copy-start | bytes 40
  7.2 104.8 %all-gather.4.cloned.1.call-start = ((), (), s32[]{:S(2)}) async-start(), calls=%async_computation.3 | async-start | bytes 12165120 | tf_op jit(solution)/shard_map/all_gather | solution.py:155
  12.6 0.7 copy-start.16
  13.4 333.0 %reduce-scatter.2.cloned.1.call-start = ((), (), s32[]{:S(2)}) async-start(), calls=%async_computation.6 | async-start | bytes 12165120 | tf_op jit(solution)/shard_map/reduce_scatter | solution.py:276
  13.5 21.5 %collective-permute-start = (bf16[512,640]{1,0:T(8,128)(2,1)S(1)}, bf16[512,640]{1,0:T(8,128)(2,1)}, u32[]{:S(2)}, u32[]{:S(2)}) collective-permute-start(bf16[512,640]{1,0:T(8,128)(2,1)S(1)} %slice.202), channel_id=1, source_target_pairs={{0,4},{4,8},{8,12},{12,16},{16,20},{20,24},{24,28},{1,5},{5,9},{9,... | collective-permute-start | bytes 1966088 | tf_op jit(solution)/shard_map/ppermute | solution.py:28
  114.5 2.3 copy-start.7
  122.7 2.2 slice-start
  123.5 2.9 slice-start.1
  124.0 3.4 slice-start.2
  131.9 1.3 copy-start.14
  139.8 0.8 copy-start.5
  155.5 1.1 copy-start.8
  188.1 2.8 copy-start.3
  190.9 2.7 copy-start.2
  193.5 2.7 copy-start.1
  196.2 1.7 copy-start.10
  200.0 146.4 %copy-start.24 = (f32[80,256]{1,0:T(8,128)S(1)}, f32[80,256]{1,0:T(8,128)}, u32[]{:S(2)}) copy-start(f32[80,256]{1,0:T(8,128)} %param.30) | copy-start | bytes 245764
  201.7 154.2 %copy-start.23 = (f32[256,80]{0,1:T(8,128)S(1)}, f32[256,80]{0,1:T(8,128)}, u32[]{:S(2)}) copy-start(f32[256,80]{0,1:T(8,128)} %param.32) | copy-start | bytes 245764
  201.7 154.9 %copy-start.21 = (f32[512,80]{0,1:T(8,128)S(1)}, f32[512,80]{0,1:T(8,128)}, u32[]{:S(2)}) copy-start(f32[512,80]{0,1:T(8,128)} %param.34) | copy-start | bytes 491524
  347.9 9.4 %copy-start.22 = (f32[80,512]{1,0:T(8,128)S(1)}, f32[80,512]{1,0:T(8,128)}, u32[]{:S(2)}) copy-start(f32[80,512]{1,0:T(8,128)} %param.31) | copy-start | bytes 491524
  354.0 0.7 copy-start.13
  354.7 3.4 copy-start.17
  358.1 6.2 %copy-start = (f32[768,640]{1,0:T(8,128)S(1)}, f32[768,640]{1,0:T(8,128)}, u32[]{:S(2)}) copy-start(f32[768,640]{1,0:T(8,128)} %add_add_fusion) | copy-start | bytes 5898244
  358.1 6.3 %copy-start.6 = (f32[256,640]{1,0:T(8,128)S(1)}, f32[256,640]{1,0:T(8,128)}, u32[]{:S(2)}) copy-start(f32[256,640]{1,0:T(8,128)} %copy-done.5) | copy-start | bytes 1966084
  359.9 61.4 %all-to-all-start = ((bf16[8,80,512]{2,1,0:T(8,128)(2,1)}), bf16[8,80,512]{2,1,0:T(8,128)(2,1)S(1)}, u32[]{:S(2)}, u32[]{:S(2)}) async-start(bf16[8,80,512]{2,1,0:T(8,128)(2,1)} %fusion.77), calls=%async_computation.1 | async-start | bytes 1310720 | tf_op jit(solution)/shard_map/all_to_all | solution.py:321
  364.3 53.8 %all-reduce.9.cloned.1.call-start = ((), (), s32[]{:S(2)}) async-start(), calls=%async_computation.5 | async-start | bytes 3932160 | tf_op jit(solution)/shard_map/psum | solution.py:293
  367.0 86.9 %all-gather.6.cloned.1.call-start = ((), (), s32[]{:S(2)}) async-start(), calls=%async_computation.4 | async-start | bytes 1638400 | tf_op jit(solution)/shard_map/all_gather | solution.py:230
  420.0 32.4 %collective-permute-start.1 = (bf16[512,640]{1,0:T(8,128)(2,1)}, bf16[512,640]{1,0:T(8,128)(2,1)}, u32[]{:S(2)}, u32[]{:S(2)}) collective-permute-start(bf16[512,640]{1,0:T(8,128)(2,1)} %slice.279), channel_id=1, source_target_pairs={{4,0},{8,4},{12,8},{16,12},{20,16},{24,20},{28,24},{5,1},{9,5},{13... | collective-permute-start | bytes 1966088 | tf_op jit(solution)/shard_map/ppermute | solution.py:28
  443.4 24.5 %all-to-all-start.1 = ((bf16[8,80,512]{2,1,0:T(8,128)(2,1)}), bf16[8,80,512]{2,1,0:T(8,128)(2,1)S(1)}, u32[]{:S(2)}, u32[]{:S(2)}) async-start(bf16[8,80,512]{2,1,0:T(8,128)(2,1)} %bitcast.61), calls=%async_computation.2 | async-start | bytes 1310720 | tf_op jit(solution)/shard_map/all_to_all | solution.py:325
  452.4 2.3 copy-start.26
  452.5 2.3 copy-start.27
  453.8 17.8 %copy-start.4 = (f32[1024,640]{1,0:T(8,128)}, f32[1024,640]{1,0:T(8,128)S(1)}, u32[]{:S(2)}) copy-start(f32[1024,640]{1,0:T(8,128)S(1)} %fusion.31) | copy-start | bytes 7864324
  453.8 15.7 %copy-start.18 = (f32[80,256]{1,0:T(8,128)S(1)}, f32[80,256]{1,0:T(8,128)}, u32[]{:S(2)}) copy-start(f32[80,256]{1,0:T(8,128)} %param.24) | copy-start | bytes 245764
  454.7 16.9 %copy-start.25 = (f32[3,128]{1,0:T(4,128)}, f32[3,128]{1,0:T(4,128)S(1)}, u32[]{:S(2)}) copy-start(f32[3,128]{1,0:T(4,128)S(1)} %slice_reduce_fusion) | copy-start | bytes 4612
  455.3 16.3 %copy-start.15 = (f32[512,80]{0,1:T(8,128)S(1)}, f32[512,80]{0,1:T(8,128)}, u32[]{:S(2)}) copy-start(f32[512,80]{0,1:T(8,128)} %param.28) | copy-start | bytes 491524
  467.9 0.9 copy-start.20
  467.9 2.3 copy-start.19
  467.9 2.9 copy-start.12
  467.9 4.4 copy-start.11
Sparse Core Ops, SparseCore 0:
  13.5 98.4 all-gather.3
  200.1 146.2 reduce-scatter.1
  368.2 49.8 all-reduce.8
  420.1 18.2 all-gather.5

commit v2 on v1

--- a/solution.py
+++ b/solution.py
@@ -1,3 +1,4 @@
+import functools
 import math
 
 import jax
@@ -100,6 +101,58 @@
         out_specs=pl.BlockSpec(memory_space=pltpu.VMEM),
         compiler_params=pltpu.CompilerParams(vmem_limit_bytes=40 * 1024 * 1024),
     )(start, block)
+
+
+def gradient_kernel(
+    head_dim,
+    normed_ref,
+    back_attn_ref,
+    ffn_in_ref,
+    back_down_ref,
+    back_query_ref,
+    attended_ref,
+    back_gate_ref,
+    back_up_ref,
+    mixed_ref,
+    back_kv_ref,
+    gain_ref,
+    grads_ref,
+):
+    def put(start, left, right):
+        product = jnp.dot(left, right, preferred_element_type=jnp.float32)
+        grads_ref[0, :, start : start + right.shape[1]] = product.astype(grads_ref.dtype)
+
+    hidden = mixed_ref.shape[2]
+    matrix_width = 2 * head_dim + 3 * hidden
+    put(0, normed_ref[:, WINDOW:], back_query_ref[0])
+    put(head_dim, back_attn_ref[...], attended_ref[0])
+    put(2 * head_dim, ffn_in_ref[...], back_gate_ref[0])
+    put(2 * head_dim + hidden, ffn_in_ref[...], back_up_ref[0])
+    put(2 * head_dim + 2 * hidden, back_down_ref[...], mixed_ref[0])
+    put(matrix_width, normed_ref[...], back_kv_ref[...])
+    grads_ref[0, :, matrix_width + back_kv_ref.shape[1] :] = gain_ref[...]
+
+
+def packed_gradients(lefts, rights, back_kv, gain_block, head_dim):
+    heads = rights[0].shape[0]
+    width = lefts[0].shape[0]
+    quarter = back_kv.shape[1] // heads
+    columns = sum(right.shape[2] for right in rights) + quarter + LANES
+    whole = [pl.BlockSpec(left.shape, lambda h: (0, 0)) for left in lefts]
+    by_head = [pl.BlockSpec((1,) + right.shape[1:], lambda h: (h, 0, 0)) for right in rights]
+    return pl.pallas_call(
+        functools.partial(gradient_kernel, head_dim),
+        grid=(heads,),
+        out_shape=jax.ShapeDtypeStruct((heads, width, columns), jnp.bfloat16),
+        in_specs=whole
+        + by_head
+        + [
+            pl.BlockSpec((back_kv.shape[0], quarter), lambda h: (0, h)),
+            pl.BlockSpec(gain_block.shape, lambda h: (0, 0)),
+        ],
+        out_specs=pl.BlockSpec((1, width, columns), lambda h: (h, 0, 0)),
+        compiler_params=pltpu.CompilerParams(vmem_limit_bytes=40 * 1024 * 1024),
+    )(*lefts, *rights, back_kv, gain_block)
 
 
 def shards(
@@ -227,16 +280,12 @@
     down_raw = ein("htf,hdf->td", mixed, down_weight)
     branch_ffn, post_norm_back = jax.vjp(rms_scale, down_raw, gain_post)
     output_own = (hidden_rows + branch_ffn).astype(low_type)
-    output = lax.all_gather(output_own, "tensor", axis=0, tiled=True)
 
     back_down_f, grad_gain_post = post_norm_back(back_out)
     back_down = back_down_f.astype(low_type)
-    grad_down = ein("td,htf->hdf", back_down, mixed)
     back_gate_f, back_up_f = activate_back(ein("td,hdf->htf", back_down, down_weight))
     back_gate = back_gate_f.astype(low_type)
     back_up = back_up_f.astype(low_type)
-    grad_gate = ein("td,htf->hdf", ffn_in, back_gate)
-    grad_up = ein("td,htf->hdf", ffn_in, back_up)
     back_ffn = ein("htf,hdf->td", back_gate, gate_weight) + ein(
         "htf,hdf->td", back_up, up_weight
     )
@@ -244,7 +293,6 @@
     back_hidden = back_out + back_pre
     back_attn_f, grad_gain_attn = attn_norm_back(back_hidden)
     back_attn = back_attn_f.astype(low_type)
-    grad_out = ein("td,htc->hdc", back_attn, attended)
     back_attended = ein("td,hdc->htc", back_attn, out_weight).astype(low_type)
     back_attended = back_attended.reshape(tensor_count * own_rows, head_dim)
     back_probs = ein("qd,kd->qk", back_attended, value_rows)
@@ -257,8 +305,6 @@
     back_query_raw = back_query_raw_f.astype(low_type)
     back_key_raw, grad_gain_key = key_back(back_keys)
     back_kv = jnp.concatenate([back_key_raw, back_values], axis=1).astype(low_type)
-    grad_query = ein("td,htc->hdc", normed, back_query_raw)
-    grad_kv = ein("td,tc->dc", normed_window, back_kv)
     back_normed = ein("tc,dc->td", back_kv, kv_weight)
     back_normed = back_normed.at[WINDOW:].add(ein("htc,hdc->td", back_query_raw, query_weight))
     back_in, grad_gain_in = input_norm_back(back_normed)
@@ -267,12 +313,14 @@
         [grad_gain_in, grad_gain_attn, grad_gain_pre, grad_gain_post, grad_gain_query, grad_gain_key]
     )
     gain_block = jax.vmap(pack_gains)(grad_gains.reshape(dp_count, gain_size))
-    gain_block = gain_block.reshape(1, width, LANES) * (1.0 / tensor_count)
-    gain_block = jnp.broadcast_to(gain_block, (tensor_count, width, LANES))
-    kv_parts = grad_kv.reshape(width, tensor_count, quarter).transpose(1, 0, 2)
-    grads = jnp.concatenate(
-        [grad_query, grad_out, grad_gate, grad_up, grad_down, kv_parts, gain_block], axis=2
-    ).astype(low_type)
+    gain_block = gain_block.reshape(width, LANES) * (1.0 / tensor_count)
+    grads = packed_gradients(
+        [normed_window.T, back_attn.T, ffn_in.T, back_down.T],
+        [back_query_raw, attended, back_gate, back_up, mixed],
+        back_kv,
+        gain_block.astype(low_type),
+        head_dim,
+    )
     summed = lax.psum_scatter(
         grads.reshape(tensor_count * width, grads.shape[2]), both, scatter_dimension=0, tiled=True
     ).astype(full_type)
@@ -286,13 +334,12 @@
     grad_kv = shared[:, :, :quarter].transpose(1, 0, 2).reshape(shard_rows, 2 * head_dim)
     grad_gains = jnp.sum(shared[:, :gain_rows, quarter:], axis=0).reshape(-1)[:gain_size]
 
-    spread = jnp.zeros((row_count + WINDOW, width), full_type)
-    spread = lax.dynamic_update_slice_in_dim(
-        spread, back_in.at[WINDOW:].add(back_hidden), first_row, 0
-    )
-    spread = lax.psum(spread.astype(low_type), "tensor")
-    behind = from_behind(spread[:WINDOW], "dp", -1).astype(full_type)
-    grad_input = spread[WINDOW:].astype(full_type).at[row_count - WINDOW :].add(behind)
+    grad_own = back_in[WINDOW:] + back_hidden
+    for part in range(WINDOW // own_rows):
+        rows = back_in[part * own_rows : (part + 1) * own_rows].astype(low_type)
+        moved = from_behind(rows, ("dp", "tensor"), part - WINDOW // own_rows)
+        grad_own = grad_own + moved.astype(full_type)
+    own_pair = jnp.concatenate([output_own, grad_own.astype(low_type)], axis=1)
 
     new_mom_query = MOMENTUM * mom_query + grad_query
     new_mom_kv = MOMENTUM * mom_kv + grad_kv
@@ -319,6 +366,9 @@
     task_count = tasks.shape[0]
     tasks = jnp.pad(tasks, ((0, dp_count - task_count), (0, 0), (0, 0)))
     mine = lax.all_to_all(tasks, "dp", split_axis=0, concat_axis=0, tiled=True)
+    mine, own_pair = lax.optimization_barrier((mine, own_pair))
+    pair = lax.all_gather(own_pair, "tensor", axis=0, tiled=True)
+    output, grad_input = pair[:, :width], pair[:, width:].astype(full_type)
     mine = mine.reshape(width, task_width).T.astype(full_type)
     paired = (dp_index == 0) | (dp_index == 4)
     steps = orthogonalize(mine, paired).T.astype(low_type).reshape(dp_count, shard_rows, task_width)

time: 485 us -> 456 us (0.940)
  the two profiles are of different devices: /device:TPU:0 before, /device:TPU:5 now
where the time goes in v2:
time: 456 us; the launch traced here: 449 us
  waiting for transfers between devices  256 us (56%)
  other arithmetic  51.1 us (11%)
  matrix products  37.1 us (8%)
  local copies, waits for them, and re-layouts  35.1 us (8%)
  starting transfers between devices  23.3 us (5%)
  Pallas kernels  20.7 us (5%)
  between operations  16.8 us (4%)
  blocking collectives  8.21 us (2%)
    reduce_scatter x1, waiting for transfers between devices, shards(): lax.psum_scatter(grads.reshape(tensor_count * width, grads.shape[2]), bot...  143 us
    all_gather x1, waiting for transfers between devices, shards(): whole = lax.all_gather(packed, both, axis=0, tiled=True)  74.7 us
    dot_general x18, matrix products, ein(): return jnp.einsum(form, left, right, preferred_element_type=full_type)  37.1 us
    unnamed x182, local copies, waits for them, and re-layouts  24.2 us
    ppermute x3, waiting for transfers between devices, from_behind(): return lax.ppermute(block, axis, route)  24.1 us
    all_to_all x1, waiting for transfers between devices, shards(): steps = lax.all_to_all(steps, 'dp', split_axis=0, concat_axis=0, tiled=True)  14.1 us
    pallas_call x1, Pallas kernels, orthogonalize(): pl.pallas_call(sweep_kernel, out_shape=jax.ShapeDtypeStruct(matrix.shape,...  14.1 us
    another operation x8, other arithmetic  9.97 us
  transfers between devices with their start and end apart: 8, of which 6 were waited for; matrix products, arithmetic and copies ran while one was open for 6% of the time, Pallas kernels for 3%

profile of v2, /device:TPU:5, one launch (start us, length us, event | category | flops | bytes accessed | tf_op | source)
XLA Modules:
  0.0 448.8 jit_solution(10609380395830175410)
XLA Ops:
  7.3 1.1 convert.78
  8.3 0.9 convert_dynamic-update-slice_fusion
  9.2 0.9 bitcast_dynamic-update-slice_fusion.1
  10.9 0.9 bitcast_dynamic-update-slice_fusion
  13.4 1.6 copy.98
  15.9 4.0 collective-permute-start
  22.5 1.3 copy.157
  23.8 0.9 copy.154
  25.2 10.2 %collective-permute-done = bf16[512,640]{0,1:T(8,128)(2,1)} collective-permute-done((bf16[512,640]{0,1:T(8,128)(2,1)}, bf16[512,640]{0,1:T(8,128)(2,1)}, u32[]{:S(2)}, u32[]{:S(2)}) %collective-permute-start) | collective-permute-done | bytes 655392 | tf_op jit(solution)/shard_map/ppermute | solution.py:29
  35.4 1.6 fusion.132
  37.3 74.7 %all-gather.4.cloned.1.call-done = bf16[2560,2304]{1,0:T(8,128)(2,1)} async-done(((bf16[80,2304]{1,0:T(8,128)(2,1)}), bf16[2560,2304]{1,0:T(8,128)(2,1)}) %all-gather.4.cloned.1.call-update) | async-done | bytes 11796496 | tf_op jit(solution)/shard_map/all_gather | solution.py:208
  111.9 0.9 slice.228
  113.6 2.0 slice_bitcast_fusion
  115.9 2.1 fusion.50
  118.1 1.7 copy.102
  120.7 1.2 copy-done.24
  122.8 2.4 fusion.87
  125.2 1.9 fusion.93
  128.5 2.1 copy-done.25
  131.3 2.0 multiply_reduce_fusion.15
  134.7 1.3 multiply_reduce_fusion.14
  136.0 2.8 fusion.8
  138.9 5.2 %fusion.22 = (bf16[4,256,512]{2,1,0:T(8,128)(2,1)S(1)}, f32[4,512,256]{1,2,0:T(8,128)}) fusion(f32[4,512,256]{1,2,0:T(8,128)S(1)} %fusion.8, bf16[4,640,2304]{2,1,0:T(8,128)(2,1)} %bitcast.216, f32[256,640]{0,1:T(8,128)S(1)} %get-tuple-element.133, f32[640]{0:T(1024)S(1)} %copy-done.52, f32[256]{0:T(256)S(1)} %fusion.123), kind=kOutput, calls=%fused_computation.32 | convolution fusion | flops 676823040 | bytes 8523264 | tf_op jit(solution)/shard_map/td,hdf->htf/dot_general | solution.py:196
  144.1 4.0 multiply_reduce_fusion.13
  148.1 1.3 copy.112
  149.5 1.0 fusion.69
  150.5 1.2 fusion.70
  151.7 4.8 %fusion.21 = (bf16[4,256,512]{2,1,0:T(8,128)(2,1)S(1)}, bf16[4,256,512]{2,1,0:T(8,128)(2,1)S(1)}) fusion(f32[4,512,256]{1,2,0:T(8,128)S(1)} %copy-done.81, f32[4,512,256]{1,2,0:T(8,128)} %get-tuple-element.169, bf16[256,640]{0,1:T(8,128)(2,1)S(1)} %fusion.70, bf16[4,640,2304]{2,1,0:T(8,128)(2,1)} %bitcast.218), kind=kOutput, calls=%fused_computation.30 | convolution fusion | flops 683671552 | bytes 9240576 | tf_op jit(solution)/shard_map/td,hdf->htf/dot_general | solution.py:196
  156.5 3.4 fusion.29
  160.0 2.8 multiply_reduce_fusion.9
  164.2 2.3 convolution_convert_fusion
  170.9 1.7 fusion.96
  174.7 0.9 copy-done.11
  175.9 2.3 fusion.90
  179.0 1.9 fusion.42
  182.3 1.2 copy-done.3
  183.5 1.2 copy-done.5
  184.7 1.2 copy-done.7
  186.0 1.0 copy-done.9
  187.0 6.6 %shard_map.302 = bf16[4,640,2304]{2,1,0:T(8,128)(2,1)} custom-call(bf16[640,768]{1,0:T(8,128)(2,1)S(1)} %fusion.152.normed_ref, bf16[640,256]{1,0:T(8,128)(2,1)S(1)} %bitcast.199, bf16[640,256]{1,0:T(8,128)(2,1)S(1)} %fusion.151.ffn_in_ref, bf16[640,256]{1,0:T(8,128)(2,1)S(1)} %bitcast.198, bf16[4,256,256]{2,1,0:T(8,128)(2,1)S(1)} %bitcast.197, ...), custom_call_target="tpu_custom_call" | custom-call | tf_op jit(solution)/shard_map/pallas_call | solution.py:143
  194.3 143.5 %reduce-scatter.2.cloned.1.call-done = bf16[80,2304]{1,0:T(8,128)(2,1)} async-done(((bf16[2560,2304]{1,0:T(8,128)(2,1)}), bf16[80,2304]{1,0:T(8,128)(2,1)}) %reduce-scatter.2.cloned.1.call-update) | async-done | bytes 368656 | tf_op jit(solution)/shard_map/reduce_scatter | solution.py:324
  337.8 1.0 convert_element_type.165
  339.6 1.5 add_convert_fusion.5
  341.1 8.2 %all-gather = f32[320,256]{1,0:T(8,128)S(1)} all-gather(f32[80,256]{1,0:T(8,128)S(1)} %get-tuple-element.155), channel_id=2, replica_groups=mesh['dp'=8,'tensor'=4] {'tensor'}, dimensions={0}, use_global_device_ids=true | all-gather | bytes 409600 | tf_op jit(solution)/shard_map/all_gather | solution.py:327
  351.0 0.9 add_convert_fusion.1
  351.9 0.9 fusion.74
  352.8 4.2 all-to-all-start
  357.0 1.7 fusion.131
  358.8 2.5 collective-permute-start.1
  361.3 2.7 collective-permute-start.2
  364.1 10.7 %collective-permute-done.1 = bf16[256,640]{0,1:T(8,128)(2,1)S(1)} collective-permute-done((bf16[256,640]{0,1:T(8,128)(2,1)S(1)}, bf16[256,640]{0,1:T(8,128)(2,1)S(1)}, u32[]{:S(2)}, u32[]{:S(2)}) %collective-permute-start.1) | collective-permute-done | bytes 327712 | tf_op jit(solution)/shard_map/ppermute | solution.py:29
  374.8 3.2 collective-permute-done.2
  378.0 1.4 fusion.77
  380.5 2.3 bitcast_convert_fusion
  382.9 1.7 copy.126
  384.6 1.3 multiply_reduce_fusion.4
  387.8 1.3 sqrt_add_fusion
  389.2 14.1 %shard_map.303 = f32[512,640]{1,0:T(8,128)S(1)} custom-call(f32[512,640]{1,0:T(8,128)S(1)} %divide_bitcast_fusion.start_ref, f32[512,512]{1,0:T(8,128)S(1)} %convert_select_fusion.block_ref), custom_call_target="tpu_custom_call" | custom-call | tf_op jit(solution)/shard_map/pallas_call | solution.py:97
  403.4 1.1 copy.127
  404.5 9.8 %all-to-all-start.1 = ((bf16[8,80,512]{2,1,0:T(8,128)(2,1)}), bf16[8,80,512]{2,1,0:T(8,128)(2,1)S(1)}, u32[]{:S(2)}, u32[]{:S(2)}) async-start(bf16[8,80,512]{2,1,0:T(8,128)(2,1)} %bitcast.53), calls=%async_computation.2 | async-start | bytes 1310720 | tf_op jit(solution)/shard_map/all_to_all | solution.py:375
  415.6 14.1 %all-to-all-done.1 = bf16[8,80,512]{2,1,0:T(8,128)(2,1)S(1)} async-done(((bf16[8,80,512]{2,1,0:T(8,128)(2,1)}), bf16[8,80,512]{2,1,0:T(8,128)(2,1)S(1)}, u32[]{:S(2)}, u32[]{:S(2)}) %all-to-all-start.1) | async-done | bytes 655392 | tf_op jit(solution)/shard_map/all_to_all | solution.py:375
  433.4 3.6 slice_convert_fusion
  437.0 3.3 copy.129
  440.3 1.4 copy.128
  (263 shorter events, 32.8 us)
Async XLA Ops:
  7.2 16.6 %copy-start = (bf16[1024,640]{1,0:T(8,128)(2,1)S(1)}, bf16[1024,640]{1,0:T(8,128)(2,1)}, u32[]{:S(2)}) copy-start(bf16[1024,640]{1,0:T(8,128)(2,1)} %param.18) | copy-start | bytes 3932164
  7.2 104.7 %all-gather.4.cloned.1.call-start = ((), (), s32[]{:S(2)}) async-start(), calls=%async_computation.3 | async-start | bytes 12165120 | tf_op jit(solution)/shard_map/all_gather | solution.py:208
  12.6 7.3 %copy-start.79 = (s32[3]{0:T(128)S(1)}, s32[3]{0:T(128)}, u32[]{:S(2)}) copy-start(s32[3]{0:T(128)} %param.19) | copy-start | bytes 40
  13.4 324.4 %reduce-scatter.2.cloned.1.call-start = ((), (), s32[]{:S(2)}) async-start(), calls=%async_computation.4 | async-start | bytes 12165120 | tf_op jit(solution)/shard_map/reduce_scatter | solution.py:324
  15.9 19.4 %collective-permute-start = (bf16[512,640]{0,1:T(8,128)(2,1)}, bf16[512,640]{0,1:T(8,128)(2,1)}, u32[]{:S(2)}, u32[]{:S(2)}) collective-permute-start(bf16[512,640]{0,1:T(8,128)(2,1)} %slice.225), channel_id=1, source_target_pairs={{0,4},{4,8},{8,12},{12,16},{16,20},{20,24},{24,28},{1,5},{5,9},{9,... | collective-permute-start | bytes 1966088 | tf_op jit(solution)/shard_map/ppermute | solution.py:29
  37.0 78.9 %copy-start.10 = (bf16[768,640]{0,1:T(8,128)(2,1)}, bf16[768,640]{0,1:T(8,128)(2,1)S(1)}, u32[]{:S(2)}) copy-start(bf16[768,640]{0,1:T(8,128)(2,1)S(1)} %get-tuple-element.135) | copy-start | bytes 2949124
  37.3 74.7 %copy-start.55 = (f32[768]{0:T(1024)}, f32[768]{0:T(1024)S(1)}, u32[]{:S(2)}) copy-start(f32[768]{0:T(1024)S(1)} %multiply_reduce_fusion.3) | copy-start | bytes 9220
  113.6 8.8 %copy-start.63 = (f32[256]{0:T(256)}, f32[256]{0:T(256)S(1)}, u32[]{:S(2)}) copy-start(f32[256]{0:T(256)S(1)} %get-tuple-element.160) | copy-start | bytes 3076
  113.6 9.0 %copy-start.61 = (f32[256]{0:T(256)}, f32[256]{0:T(256)S(1)}, u32[]{:S(2)}) copy-start(f32[256]{0:T(256)S(1)} %get-tuple-element.161) | copy-start | bytes 3076
  118.0 4.6 %copy-start.17 = (f32[4,256,256]{1,2,0:T(8,128)}, f32[4,256,256]{1,2,0:T(8,128)S(1)}, u32[]{:S(2)}) copy-start(f32[4,256,256]{1,2,0:T(8,128)S(1)} %get-tuple-element.163) | copy-start | bytes 3145732
  118.0 2.6 copy-start.59
  122.4 2.9 copy-start.57
  122.6 2.7 copy-start.50
  122.6 4.6 %copy-start.29 = (pred[96,8,4,256]{3,1,2,0:T(8,128)(4,1)S(1)}, pred[96,8,4,256]{3,1,2,0:T(8,128)(4,1)}, u32[]{:S(2)}) copy-start(pred[96,8,4,256]{3,1,2,0:T(8,128)(4,1)} %copy.157) | copy-start | bytes 2359300
  125.2 2.7 copy-start.36
  128.0 3.3 copy-start.15
  128.0 3.3 copy-start.65
  128.0 2.5 copy-start.25
  134.1 1.9 copy-start.52
  136.0 26.8 %copy-start.70 = (f32[256]{0:T(256)}, f32[256]{0:T(256)S(1)}, u32[]{:S(2)}) copy-start(f32[256]{0:T(256)S(1)} %fusion.123) | copy-start | bytes 3076
  138.9 5.3 %copy-start.80 = (f32[4,512,256]{1,2,0:T(8,128)}, f32[4,512,256]{1,2,0:T(8,128)S(1)}, u32[]{:S(2)}) copy-start(f32[4,512,256]{1,2,0:T(8,128)S(1)} %fusion.8) | copy-start | bytes 6291460
  144.1 4.0 copy-start.2
  144.1 5.4 %copy-start.22 = (bf16[256,640]{0,1:T(8,128)(2,1)S(1)}, bf16[256,640]{0,1:T(8,128)(2,1)}, u32[]{:S(2)}) copy-start(bf16[256,640]{0,1:T(8,128)(2,1)} %copy.154) | copy-start | bytes 983044
  144.1 5.4 %copy-start.54 = (f32[640]{0:T(1024)S(1)}, f32[640]{0:T(1024)}, u32[]{:S(2)}) copy-start(f32[640]{0:T(1024)} %get-tuple-element.156) | copy-start | bytes 7684
  149.5 2.2 copy-start.81
  156.5 3.4 copy-start.6
  156.5 3.4 copy-start.4
  159.9 2.8 copy-start.23
  160.0 2.8 copy-start.47
  162.8 3.7 copy-start.26
  163.4 3.1 copy-start.16
  163.4 3.1 copy-start.66
  163.4 3.1 copy-start.68
  170.2 2.4 copy-start.64
  170.9 2.1 copy-start.58
  174.4 1.5 copy-start.49
  175.6 2.6 copy-start.18
  175.6 2.6 copy-start.62
  175.9 2.7 copy-start.60
  180.9 1.3 copy-start.13
  180.9 1.3 copy-start.69
  182.3 1.2 copy-start.3
  193.6 145.3 %copy-start.45 = (f32[256,80]{0,1:T(8,128)S(1)}, f32[256,80]{0,1:T(8,128)}, u32[]{:S(2)}) copy-start(f32[256,80]{0,1:T(8,128)} %param.28) | copy-start | bytes 245764
  193.7 145.9 %copy-start.46 = (f32[80,256]{1,0:T(8,128)S(1)}, f32[80,256]{1,0:T(8,128)}, u32[]{:S(2)}) copy-start(f32[80,256]{1,0:T(8,128)} %param.26) | copy-start | bytes 245764
  193.7 155.7 %copy-start.43 = (f32[512,80]{0,1:T(8,128)S(1)}, f32[512,80]{0,1:T(8,128)}, u32[]{:S(2)}) copy-start(f32[512,80]{0,1:T(8,128)} %param.30) | copy-start | bytes 491524
  194.3 155.8 %copy-start.44 = (f32[80,512]{1,0:T(8,128)S(1)}, f32[80,512]{1,0:T(8,128)}, u32[]{:S(2)}) copy-start(f32[80,512]{1,0:T(8,128)} %param.27) | copy-start | bytes 491524
  338.9 12.1 %copy-start.33 = (f32[2,80,512]{2,1,0:T(8,128)S(1)}, f32[2,80,512]{2,1,0:T(8,128)}, u32[]{:S(2)}) copy-start(f32[2,80,512]{2,1,0:T(8,128)} %param.29) | copy-start | bytes 983044
  350.9 6.1 %copy-start.12 = (bf16[768,640]{0,1:T(8,128)(2,1)S(1)}, bf16[768,640]{0,1:T(8,128)(2,1)}, u32[]{:S(2)}) copy-start(bf16[768,640]{0,1:T(8,128)(2,1)} %copy-done.10) | copy-start | bytes 2949124
  350.9 6.1 %copy-start.14 = (f32[768,640]{0,1:T(8,128)S(1)}, f32[768,640]{0,1:T(8,128)}, u32[]{:S(2)}) copy-start(f32[768,640]{0,1:T(8,128)} %copy-done.13) | copy-start | bytes 5898244
  352.8 27.6 %all-to-all-start = ((bf16[8,80,512]{2,1,0:T(8,128)(2,1)}), bf16[8,80,512]{2,1,0:T(8,128)(2,1)}, u32[]{:S(2)}, u32[]{:S(2)}) async-start(bf16[8,80,512]{2,1,0:T(8,128)(2,1)} %fusion.74), calls=%async_computation.1 | async-start | bytes 1310720 | tf_op jit(solution)/shard_map/all_to_all | solution.py:368
  357.0 76.4 %all-gather.6.cloned.1.call-start = ((), (), s32[]{:S(2)}) async-start(), calls=%async_computation.5 | async-start | bytes 3276800 | tf_op jit(solution)/shard_map/all_gather | solution.py:370
  358.8 20.7 %copy-start.27 = (bf16[256,640]{0,1:T(8,128)(2,1)S(1)}, bf16[256,640]{0,1:T(8,128)(2,1)}, u32[]{:S(2)}) copy-start(bf16[256,640]{0,1:T(8,128)(2,1)} %get-tuple-element.154) | copy-start | bytes 983044
  358.8 16.0 %collective-permute-start.1 = (bf16[256,640]{0,1:T(8,128)(2,1)S(1)}, bf16[256,640]{0,1:T(8,128)(2,1)S(1)}, u32[]{:S(2)}, u32[]{:S(2)}) collective-permute-start(bf16[256,640]{0,1:T(8,128)(2,1)S(1)} %get-tuple-element.146), channel_id=1, source_target_pairs={{2,0},{3,1},{4,2},{5,3},{6,4},{7,5},{8,6},{9,7},{10,8},{11,9},{12,... | collective-permute-start | bytes 983048 | tf_op jit(solution)/shard_map/ppermute | solution.py:29
  361.3 16.7 %collective-permute-start.2 = (bf16[256,640]{0,1:T(8,128)(2,1)S(1)}, bf16[256,640]{0,1:T(8,128)(2,1)S(1)}, u32[]{:S(2)}, u32[]{:S(2)}) collective-permute-start(bf16[256,640]{0,1:T(8,128)(2,1)S(1)} %get-tuple-element.147), channel_id=1, source_target_pairs={{1,0},{2,1},{3,2},{4,3},{5,4},{6,5},{7,6},{8,7},{9,8},{10,9},{11,1... | collective-permute-start | bytes 983048 | tf_op jit(solution)/shard_map/ppermute | solution.py:29
  403.3 11.8 %copy-start.75 = (f32[384]{0:T(512)S(1)}, f32[384]{0:T(512)}, u32[]{:S(2)}) copy-start(f32[384]{0:T(512)} %param.25) | copy-start | bytes 4612
  403.3 11.7 %copy-start.78 = (f32[384]{0:T(512)S(1)}, f32[384]{0:T(512)}, u32[]{:S(2)}) copy-start(f32[384]{0:T(512)} %param.31) | copy-start | bytes 4612
  404.5 25.4 %copy-start.34 = (f32[256,80]{0,1:T(8,128)S(1)}, f32[256,80]{0,1:T(8,128)}, u32[]{:S(2)}) copy-start(f32[256,80]{0,1:T(8,128)} %param.22) | copy-start | bytes 245764
  404.5 26.1 %copy-start.35 = (f32[80,256]{1,0:T(8,128)S(1)}, f32[80,256]{1,0:T(8,128)}, u32[]{:S(2)}) copy-start(f32[80,256]{1,0:T(8,128)} %param.20) | copy-start | bytes 245764
  404.5 26.7 %copy-start.31 = (f32[512,80]{0,1:T(8,128)S(1)}, f32[512,80]{0,1:T(8,128)}, u32[]{:S(2)}) copy-start(f32[512,80]{0,1:T(8,128)} %param.24) | copy-start | bytes 491524
  404.5 27.4 %copy-start.38 = (f32[80,512]{1,0:T(8,128)S(1)}, f32[80,512]{1,0:T(8,128)}, u32[]{:S(2)}) copy-start(f32[80,512]{1,0:T(8,128)} %param.21) | copy-start | bytes 491524
  404.5 25.2 %all-to-all-start.1 = ((bf16[8,80,512]{2,1,0:T(8,128)(2,1)}), bf16[8,80,512]{2,1,0:T(8,128)(2,1)S(1)}, u32[]{:S(2)}, u32[]{:S(2)}) async-start(bf16[8,80,512]{2,1,0:T(8,128)(2,1)} %bitcast.53), calls=%async_computation.2 | async-start | bytes 1310720 | tf_op jit(solution)/shard_map/all_to_all | solution.py:375
  414.3 18.4 %copy-start.28 = (f32[2,80,512]{2,1,0:T(8,128)S(1)}, f32[2,80,512]{2,1,0:T(8,128)}, u32[]{:S(2)}) copy-start(f32[2,80,512]{2,1,0:T(8,128)} %param.23) | copy-start | bytes 983044
  415.0 18.4 %copy-start.74 = (f32[3,128]{1,0:T(4,128)}, f32[3,128]{1,0:T(4,128)S(1)}, u32[]{:S(2)}) copy-start(f32[3,128]{1,0:T(4,128)S(1)} %slice_reduce_fusion) | copy-start | bytes 4612
  437.0 4.8 %copy-start.1 = (bf16[1024,640]{1,0:T(8,128)(2,1)S(1)}, bf16[1024,640]{1,0:T(8,128)(2,1)}, u32[]{:S(2)}) copy-start(bf16[1024,640]{1,0:T(8,128)(2,1)} %param.18) | copy-start | bytes 3932164
  (26 other events, 22.7 us)
Sparse Core Ops, SparseCore 0:
  13.5 98.3 all-gather.3
  193.8 143.9 reduce-scatter.1
  380.5 29.8 all-gather.5
